TPU v7x, 32 devices: a whole 2x2x4 slice. The times are simulated.
32 devices in a mesh: row: 4 (over y, x), col: 8 (over z, core).
Axes of the slice: x: 2, y: 2, z: 4, core: 2. Of those that a mesh axis runs over, the one named last changes fastest.
Arguments:
- tokens: bfloat16 [12608, 512], P('col', 'row'), may hold values from -3 to 3
- ln1_gain: float32 [512], P('row'), may hold values from 0.5 to 1.5
- ln1_bias: float32 [512], P('row'), may hold values from -1.5 to 1.5
- qkv_weight: bfloat16 [512, 1536], P('row', 'col'), may hold values from -0.25 to 0.25
- out_weight: bfloat16 [512, 512], P('row', 'col'), may hold values from -1 to 1
- ln2_gain: float32 [512], P('row'), may hold values from 0.5 to 1.5
- ln2_bias: float32 [512], P('row'), may hold values from -1.5 to 1.5
- router_weight: bfloat16 [512, 32], P('row'), may hold values from -0.1875 to 0.1875
- expert_in: bfloat16 [32, 512, 2048], P(None, 'row', 'col'), may hold values from -0.25 to 0.25
- expert_out: bfloat16 [32, 2048, 512], P(None, 'row', 'col'), may hold values from -2 to 2
- routes: int32 [12608, 2], P('col'), may hold values from 0 to 31, all different within a row; in each aligned block of 1576 rows (0 to 1575, 1576 to 3151, ...) at most 120 rows name the same one
- keep: int32 [12608, 2], P('col'), may hold values 0 or 1
- cotangent: bfloat16 [12608, 512], P('col', 'row'), may hold values from -6 to 6
Outputs:
- layer_out: bfloat16 [12608, 512], P('col', 'row')
- tokens_grad: float32 [12608, 512], P('col', 'row')
- ln1_gain_grad: float32 [512], P(('row', 'col'))
- ln1_bias_grad: float32 [512], P(('row', 'col'))
- qkv_grad: float32 [512, 1536], P('row', 'col')
- out_weight_grad: float32 [512, 512], P('row', 'col')
- ln2_gain_grad: float32 [512], P(('row', 'col'))
- ln2_bias_grad: float32 [512], P(('row', 'col'))
- router_grad: float32 [512, 32], P(('row', 'col'))
- expert_in_grad: float32 [32, 512, 2048], P(None, 'row', 'col')
- expert_out_grad: float32 [32, 2048, 512], P(None, 'row', 'col')
Inputs may be any that keep to these rules, and one draw needn't show every extreme that they name: `routes`: each row names two different experts. In each aligned block of 1576 rows no expert is named by more than 120 rows, and in some block some expert is named by exactly 120 rows.
All inputs are finite; a program needn't handle non-finite values. No bound on the sum of `keep` on one device may be relied on, other than what follows from the above.
Results may differ from a plain program's by a relative error of at most 0.019.
Values may be sent and summed in bfloat16 or wider, within the bound.
No kernel may reach another device: no remote copies, remote signals or barrier semaphores. Data moves between devices by JAX's collectives and lax.ppermute only.
A program may use at most 192 MiB of HBM per device.

v0:
```python
from functools import partial

import jax
import jax.numpy as jnp
from jax import lax
from jax.sharding import PartitionSpec as P

E = 32
SEQ = 197
HD = 64
CAP = 120


EPS_NORM = 1e-06


def row_totals(pieces):
    return lax.psum(pieces, "row")


def attention_weights(qkv_weight, out_weight):
    return (
        lax.all_gather(qkv_weight, "col", axis=1, tiled=True),
        lax.all_gather(out_weight, "col", axis=1, tiled=True),
    )


def expert_weights(expert_in, expert_out):
    return (
        lax.all_gather(expert_in, "col", axis=2, tiled=True),
        lax.all_gather(expert_out, "col", axis=2, tiled=True),
    )


def normalize(values):
    features = values.shape[1] * lax.axis_size("row")
    (sums,) = row_totals((jnp.sum(values, axis=1),))
    average = sums / features
    centred = values - average[:, None]
    (squares,) = row_totals((jnp.sum(centred * centred, axis=1),))
    variance = squares / features
    inverse = lax.rsqrt(variance + EPS_NORM)
    return (centred * inverse[:, None], inverse)


def norm_backward(grad_normed, normalized, inverse, ln_gain):
    features = normalized.shape[1] * lax.axis_size("row")
    scaled = grad_normed * ln_gain
    sum_plain, sum_cross = row_totals(
        (jnp.sum(scaled, axis=1), jnp.sum(scaled * normalized, axis=1))
    )
    return inverse[:, None] * (
        scaled - sum_plain[:, None] / features - normalized * (sum_cross[:, None] / features)
    )


def softmax_last(scores):
    top_value = jnp.max(scores, axis=-1, keepdims=True)
    powers = jnp.exp(scores - top_value)
    return powers / jnp.sum(powers, axis=-1, keepdims=True)


def slot_tables(route_block, keep_block):
    pair_ids = route_block.reshape(-1)
    pair_count = pair_ids.shape[0]
    onehot = (pair_ids[:, None] == jnp.arange(E, dtype=jnp.int32)[None, :]).astype(jnp.int32)
    running = jnp.cumsum(onehot, axis=0)
    slot_of_pair = pair_ids * CAP + jnp.sum(running * onehot, axis=1) - 1
    pair_of_slot = (
        jnp.full((E * CAP,), pair_count, jnp.int32)
        .at[slot_of_pair]
        .set(jnp.arange(pair_count, dtype=jnp.int32))
    )
    keep_ext = jnp.concatenate([keep_block.reshape(-1), jnp.zeros((1,), jnp.int32)])
    slot_keep = keep_ext[pair_of_slot]
    token_of_slot = jnp.minimum(pair_of_slot // 2, pair_count // 2 - 1)
    return (slot_of_pair, pair_of_slot, slot_keep, token_of_slot)


def local(
    tokens,
    ln1_gain,
    ln1_bias,
    qkv_weight,
    out_weight,
    ln2_gain,
    ln2_bias,
    router_weight,
    expert_in,
    expert_out,
    routes,
    keep,
    cotangent,
):
    block_tok = tokens.shape[0]
    width_part = tokens.shape[1]
    width = width_part * lax.axis_size("row")
    images = block_tok // SEQ
    heads_part = width_part // HD
    score_scale = HD ** (-0.5)
    slot_of_pair, pair_of_slot, slot_keep, token_of_slot = slot_tables(routes, keep)
    tok_float = tokens.astype(jnp.float32)
    normal1, inverse1 = normalize(tok_float)
    normed1 = (normal1 * ln1_gain + ln1_bias).astype(jnp.bfloat16)
    qkv_all, out_all = attention_weights(qkv_weight, out_weight)
    partial_qkv = jnp.dot(normed1, qkv_all, preferred_element_type=jnp.float32).reshape(
        block_tok, 3, width
    )
    project = lax.psum_scatter(partial_qkv, "row", scatter_dimension=2, tiled=True).astype(
        jnp.bfloat16
    )
    split_heads = project.reshape(images, SEQ, 3, heads_part, HD)
    queries = split_heads[:, :, 0]
    keys_all = split_heads[:, :, 1]
    values_all = split_heads[:, :, 2]
    scores = (
        jnp.einsum("bqhd,bkhd->bhqk", queries, keys_all, preferred_element_type=jnp.float32)
        * score_scale
    )
    top_value = jnp.max(scores, axis=-1, keepdims=True)
    powers = jnp.exp(scores - top_value)
    power_sums = jnp.sum(powers, axis=-1, keepdims=True)
    log_total = top_value + jnp.log(power_sums)
    attn_probs = (powers / power_sums).astype(jnp.bfloat16)
    attended = jnp.einsum(
        "bhqk,bkhd->bqhd", attn_probs, values_all, preferred_element_type=jnp.float32
    )
    attended = attended.reshape(block_tok, width_part).astype(jnp.bfloat16)
    partial_mix = jnp.dot(attended, out_all, preferred_element_type=jnp.float32)
    attn_out = lax.psum_scatter(partial_mix, "row", scatter_dimension=1, tiled=True)
    residual = tok_float + attn_out
    normal2, inverse2 = normalize(residual)
    normed2 = (normal2 * ln2_gain + ln2_bias).astype(jnp.bfloat16)
    logits = lax.psum(jnp.dot(normed2, router_weight, preferred_element_type=jnp.float32), "row")
    gate_probs = softmax_last(logits)
    onehot = (routes[:, :, None] == jnp.arange(E, dtype=jnp.int32)[None, None, :]).astype(
        jnp.float32
    )
    keep_float = keep.astype(jnp.float32)
    chosen = jnp.sum(onehot * gate_probs[:, None, :], axis=2) * keep_float
    dispatched = (normed2[token_of_slot] * slot_keep.astype(jnp.bfloat16)[:, None]).reshape(
        E, CAP, width_part
    )
    expert_pair = expert_weights(expert_in, expert_out)
    partial_hidden = jnp.einsum(
        "ecd,edh->ech", dispatched, expert_pair[0], preferred_element_type=jnp.float32
    )
    pre_act = lax.psum_scatter(
        partial_hidden.astype(jnp.bfloat16), "row", scatter_dimension=2, tiled=True
    ).astype(jnp.float32)
    activated = jax.nn.gelu(pre_act, approximate=False).astype(jnp.bfloat16)
    partial_res = jnp.einsum(
        "ech,ehd->ecd", activated, expert_pair[1], preferred_element_type=jnp.float32
    )
    expert_res = (
        lax.psum_scatter(partial_res.astype(jnp.bfloat16), "row", scatter_dimension=2, tiled=True)
        .astype(jnp.float32)
        .reshape(E * CAP, width_part)
    )
    picked = expert_res[slot_of_pair].reshape(block_tok, 2, width_part)
    layer_out = (residual + jnp.sum(chosen[:, :, None] * picked, axis=1)).astype(jnp.bfloat16)
    grad_out = cotangent.astype(jnp.float32)
    qkv_back, out_back = attention_weights(qkv_weight, out_weight)
    in_back, res_back = expert_weights(expert_in, expert_out)
    (grad_chosen,) = row_totals((jnp.sum(grad_out[:, None, :] * picked, axis=2),))
    grad_gate = jnp.sum(onehot * (keep_float * grad_chosen)[:, :, None], axis=1)
    grad_logits = (
        gate_probs * (grad_gate - jnp.sum(gate_probs * grad_gate, axis=1, keepdims=True))
    ).astype(jnp.bfloat16)
    chosen_ext = jnp.concatenate([chosen.reshape(-1), jnp.zeros((1,), jnp.float32)])
    grad_res = (chosen_ext[pair_of_slot][:, None] * grad_out[token_of_slot]).astype(jnp.bfloat16)
    gelu_back = jax.vjp(partial(jax.nn.gelu, approximate=False), pre_act)[1]
    grad_res_full = lax.all_gather(grad_res.reshape(E, CAP, width_part), "row", axis=2, tiled=True)
    grad_act = jnp.einsum(
        "ecd,ehd->ech", grad_res_full, res_back, preferred_element_type=jnp.float32
    )
    out_expert_grad = jnp.einsum(
        "ech,ecd->ehd", activated, grad_res_full, preferred_element_type=jnp.float32
    )
    (grad_pre,) = gelu_back(grad_act)
    grad_pre_full = lax.all_gather(grad_pre.astype(jnp.bfloat16), "row", axis=2, tiled=True)
    grad_disp = jnp.einsum(
        "ech,edh->ecd", grad_pre_full, in_back, preferred_element_type=jnp.float32
    ).reshape(E * CAP, width_part)
    in_expert_grad = jnp.einsum(
        "ecd,ech->edh", dispatched, grad_pre_full, preferred_element_type=jnp.float32
    )
    in_grad_part, res_grad_part = (
        lax.psum_scatter(in_expert_grad, "col", scatter_dimension=2, tiled=True),
        lax.psum_scatter(out_expert_grad, "col", scatter_dimension=2, tiled=True),
    )
    picked_grad = grad_disp[slot_of_pair].reshape(block_tok, 2, width_part)
    grad_norm2 = jnp.sum(keep_float[:, :, None] * picked_grad, axis=1) + jnp.dot(
        grad_logits, router_weight.T, preferred_element_type=jnp.float32
    )
    router_part = jnp.dot(normed2.T, grad_logits, preferred_element_type=jnp.float32)
    gain2_part = jnp.sum(grad_norm2 * normal2, axis=0)
    bias2_part = jnp.sum(grad_norm2, axis=0)
    grad_resid = grad_out + norm_backward(grad_norm2, normal2, inverse2, ln2_gain)
    grad_attn_full = lax.all_gather(grad_resid.astype(jnp.bfloat16), "row", axis=1, tiled=True)
    out_weight_part = jnp.dot(attended.T, grad_attn_full, preferred_element_type=jnp.float32)
    grad_attended = jnp.dot(grad_attn_full, out_back.T, preferred_element_type=jnp.float32).astype(
        jnp.bfloat16
    )
    grad_heads = grad_attended.reshape(images, SEQ, heads_part, HD)
    again_scores = (
        jnp.einsum("bqhd,bkhd->bhqk", queries, keys_all, preferred_element_type=jnp.float32)
        * score_scale
    )
    float_probs = jnp.exp(again_scores - log_total)
    grad_values = jnp.einsum(
        "bhqk,bqhd->bkhd",
        float_probs.astype(jnp.bfloat16),
        grad_heads,
        preferred_element_type=jnp.float32,
    )
    grad_probs = jnp.einsum(
        "bqhd,bkhd->bhqk", grad_heads, values_all, preferred_element_type=jnp.float32
    )
    row_dot = jnp.sum(float_probs * grad_probs, axis=-1, keepdims=True)
    grad_scores = (float_probs * (grad_probs - row_dot)).astype(jnp.bfloat16)
    grad_queries = (
        jnp.einsum("bhqk,bkhd->bqhd", grad_scores, keys_all, preferred_element_type=jnp.float32)
        * score_scale
    )
    grad_keys = (
        jnp.einsum("bhqk,bqhd->bkhd", grad_scores, queries, preferred_element_type=jnp.float32)
        * score_scale
    )
    grad_project = (
        jnp.stack([grad_queries, grad_keys, grad_values], axis=2)
        .reshape(block_tok, 3, width_part)
        .astype(jnp.bfloat16)
    )
    grad_project_full = lax.all_gather(grad_project, "row", axis=2, tiled=True).reshape(
        block_tok, 3 * width
    )
    qkv_weight_part = jnp.dot(normed1.T, grad_project_full, preferred_element_type=jnp.float32)
    grad_norm1 = jnp.dot(grad_project_full, qkv_back.T, preferred_element_type=jnp.float32)
    gain1_part = jnp.sum(grad_norm1 * normal1, axis=0)
    bias1_part = jnp.sum(grad_norm1, axis=0)
    tokens_grad = grad_resid + norm_backward(grad_norm1, normal1, inverse1, ln1_gain)
    small_part = jnp.concatenate(
        [router_part.T, jnp.stack([gain1_part, bias1_part, gain2_part, bias2_part], axis=0)], axis=0
    )
    qkv_grad, out_grad, small_grad = (
        lax.psum_scatter(qkv_weight_part, "col", scatter_dimension=1, tiled=True),
        lax.psum_scatter(out_weight_part, "col", scatter_dimension=1, tiled=True),
        lax.psum_scatter(small_part, "col", scatter_dimension=1, tiled=True),
    )
    return (
        layer_out,
        tokens_grad,
        small_grad[E],
        small_grad[E + 1],
        qkv_grad,
        out_grad,
        small_grad[E + 2],
        small_grad[E + 3],
        small_grad[:E].T,
        in_grad_part,
        res_grad_part,
    )


def solution(mesh):
    in_specs = (
        P("col", "row"),
        P("row"),
        P("row"),
        P("row", "col"),
        P("row", "col"),
        P("row"),
        P("row"),
        P("row", None),
        P(None, "row", "col"),
        P(None, "row", "col"),
        P("col", None),
        P("col", None),
        P("col", "row"),
    )
    out_specs = (
        P("col", "row"),
        P("col", "row"),
        P(("row", "col")),
        P(("row", "col")),
        P("row", "col"),
        P("row", "col"),
        P(("row", "col")),
        P(("row", "col")),
        P(("row", "col"), None),
        P(None, "row", "col"),
        P(None, "row", "col"),
    )
    return jax.shard_map(local, mesh=mesh, in_specs=in_specs, out_specs=out_specs, check_vma=False)
```

profile of v0, /device:TPU:0, one launch (start us, length us, event | category | flops | bytes accessed | tf_op | source)
XLA Modules:
  0.0 1786.2 jit_solution(3690590149422040532)
XLA Ops:
  9.3 11.5 psum.70
  22.4 8.2 psum.71
  30.5 15.1 all_gather.28
  46.4 6.5 fusion.90
  53.6 13.9 all_gather.29
  67.6 86.9 %reduce-scatter.14.cloned.1.call-done = f32[1576,3,128]{0,2,1:T(8,128)} async-done(((f32[1576,3,512]{0,2,1:T(8,128)}), f32[1576,3,128]{0,2,1:T(8,128)}) %reduce-scatter.14.cloned.1.call-update) | async-done | bytes 2420752 | tf_op jit(solution)/shard_map/reduce_scatter | solution.py:109
  165.5 45.7 %reduce-scatter.16.cloned.1.call-done = f32[1576,128]{1,0:T(8,128)} async-done(((f32[1576,512]{1,0:T(8,128)}), f32[1576,128]{1,0:T(8,128)}) %reduce-scatter.16.cloned.1.call-update) | async-done | bytes 806928 | tf_op jit(solution)/shard_map/reduce_scatter | solution.py:130
  212.7 9.1 psum.72
  222.3 8.8 psum.73
  235.8 9.2 reduce-window.6
  246.6 15.8 scatter_custom_fusion
  262.6 6.2 gather_fusion.4
  268.8 6.6 all-reduce.5.cloned.1.call-done
  281.3 20.1 %gather_fusion.3 = f32[3840]{0:T(1024)S(1)} fusion(f32[3153]{0:T(1024)S(1)} %pad_maximum_fusion.1, s32[4096]{0:T(1024)S(1)} %pad_clamp_fusion.1), kind=kCustom, calls=%fused_computation.3 | custom fusion | bytes 46080 | tf_op jit(solution)/shard_map/gather | solution.py:171
  303.9 20.2 %gather_fusion.1 = s32[3840]{0:T(1024)S(1)} fusion(s32[3153]{0:T(1024)S(1)} %pad_add_fusion, s32[4096]{0:T(1024)S(1)} %pad_clamp_fusion.1), kind=kCustom, calls=%fused_computation.1 | custom fusion | bytes 46080 | tf_op jit(solution)/shard_map/gather | solution.py:75
  324.2 7.5 gather_fusion
  331.7 54.8 %all-gather.7.cloned.1.call-done = bf16[32,128,2048]{2,1,0:T(8,128)(2,1)} async-done(((bf16[32,128,256]{2,1,0:T(8,128)(2,1)}), bf16[32,128,2048]{2,1,0:T(8,128)(2,1)}) %all-gather.7.cloned.1.call-update) | async-done | bytes 16777232 | tf_op jit(solution)/shard_map/all_gather | solution.py:30
  386.4 13.3 convolution_convert_fusion
  400.0 137.1 %all-gather.9.cloned.1.call-done = bf16[32,512,512]{1,2,0:T(8,128)(2,1)} async-done(((bf16[32,512,64]{1,2,0:T(8,128)(2,1)}), bf16[32,512,512]{1,2,0:T(8,128)(2,1)}) %all-gather.9.cloned.1.call-update) | async-done | bytes 16777232 | tf_op jit(solution)/shard_map/all_gather | solution.py:31
  537.1 50.8 %all-gather.11.cloned.1.call-done = bf16[32,120,512]{2,1,0:T(8,128)(2,1)} async-done(((bf16[32,120,128]{2,1,0:T(8,128)(2,1)}), bf16[32,120,512]{2,1,0:T(8,128)(2,1)}) %all-gather.11.cloned.1.call-update) | async-done | bytes 3932176 | tf_op jit(solution)/shard_map/all_gather | solution.py:173
  587.9 24.3 %fusion.8 = (bf16[32,120,512]{2,1,0:T(8,128)(2,1)}, f32[32,120,512]{2,1,0:T(8,128)}) fusion(bf16[32,120,512]{2,1,0:T(8,128)(2,1)} %reduce-scatter.18.cloned.1.call-done, bf16[32,120,512]{2,1,0:T(8,128)(2,1)} %all-gather.11.cloned.1.call-done, bf16[32,512,512]{1,2,0:T(8,128)(2,1)} %all-gather.9.cloned.1.call-done), kind=kOutput, calls=%fused_computation.19 | convolution fusion | flops 2156789760 | bytes 36438016 | tf_op jit(solution)/shard_map/ecd,ehd->ech/dot_general | solution.py:174
  612.2 13.9 convolution_convert_fusion.1
  626.1 7.8 copy.113
  633.9 9.0 reshape.253
  645.2 170.3 %reduce-scatter.28.cloned.1.call-done = bf16[128,3840]{1,0:T(8,128)(2,1)} async-done(((bf16[512,3840]{1,0:T(8,128)(2,1)}), bf16[128,3840]{1,0:T(8,128)(2,1)}) %reduce-scatter.28.cloned.1.call-update) | async-done | bytes 983056
  815.6 3.8 reshape.254
  822.5 7.0 gather_fusion.2
  829.5 12.8 multiply_reduce_fusion.2
  842.5 15.7 psum.75
  858.5 12.6 fusion.102
  871.1 7.0 gather_fusion.5
  878.1 9.8 multiply_reduce_fusion.3
  887.9 3.5 multiply_reduce_fusion.5
  891.5 15.3 all-reduce.2
  907.5 3.5 fusion.95
  912.0 30.4 %all-gather.15.cloned.1.call-done = bf16[1576,512]{1,0:T(8,128)(2,1)} async-done(((bf16[1576,128]{1,0:T(8,128)(2,1)}), bf16[1576,512]{1,0:T(8,128)(2,1)}) %all-gather.15.cloned.1.call-update) | async-done | bytes 1613840 | tf_op jit(solution)/shard_map/all_gather | solution.py:200
  942.4 2.7 convolution_convert_fusion.2
  945.1 2.8 reshape.257
  947.9 3.0 copy.99
  964.5 60.2 %all-gather.17.cloned.1.call-done = bf16[1576,3,512]{0,2,1:T(8,128)(2,1)} async-done(((bf16[1576,3,128]{0,2,1:T(8,128)(2,1)}), bf16[1576,3,512]{0,2,1:T(8,128)(2,1)}) %all-gather.17.cloned.1.call-update) | async-done | bytes 4841488 | tf_op jit(solution)/shard_map/all_gather | solution.py:235
  1024.8 5.7 fusion.71
  1033.1 5.0 fusion.88
  1038.2 17.3 fusion.92
  1056.7 16.9 fusion.62
  1073.6 15.2 all-reduce.1
  1095.4 29.7 %reduce-scatter.20.cloned.1.call-done = f32[128,192]{0,1:T(8,128)} async-done(((f32[128,1536]{0,1:T(8,128)}), f32[128,192]{0,1:T(8,128)}) %reduce-scatter.20.cloned.1.call-update) | async-done | bytes 98320 | tf_op jit(solution)/shard_map/reduce_scatter | solution.py:247
  1125.1 326.5 %reduce-scatter.26.cloned.1.call-done = f32[32,512,64]{1,2,0:T(8,128)} async-done(((f32[32,512,512]{1,2,0:T(8,128)}), f32[32,512,64]{1,2,0:T(8,128)}) %reduce-scatter.26.cloned.1.call-update) | async-done | bytes 4194320 | tf_op jit(solution)/shard_map/reduce_scatter | solution.py:190
  1451.6 326.8 %reduce-scatter.24.cloned.1.call-done = f32[32,128,256]{2,1,0:T(8,128)} async-done(((f32[32,128,2048]{2,1,0:T(8,128)}), f32[32,128,256]{2,1,0:T(8,128)}) %reduce-scatter.24.cloned.1.call-update) | async-done | bytes 4194320 | tf_op jit(solution)/shard_map/reduce_scatter | solution.py:189
  (220 shorter events, 63.1 us)
Async XLA Ops:
  8.0 223.7 %copy-start = (bf16[128,32]{0,1:T(8,128)(2,1)S(1)}, bf16[128,32]{0,1:T(8,128)(2,1)}, u32[]{:S(2)}) copy-start(bf16[128,32]{0,1:T(8,128)(2,1)} %param.20) | copy-start | bytes 24580
  8.0 146.5 %reduce-scatter.14.cloned.1.call-start = ((), (), s32[]{:S(2)}) async-start(), calls=%async_computation.9 | async-start | bytes 12779520 | tf_op jit(solution)/shard_map/reduce_scatter | solution.py:109
  20.8 32.1 %copy-start.31 = (f32[1576]{0:T(1024)}, f32[1576]{0:T(1024)S(1)}, u32[]{:S(2)}) copy-start(f32[1576]{0:T(1024)S(1)} %broadcast_multiply_fusion.6) | copy-start | bytes 18916
  30.5 22.4 %copy-start.37 = (f32[1576]{0:T(1024)}, f32[1576]{0:T(1024)S(1)}, u32[]{:S(2)}) copy-start(f32[1576]{0:T(1024)S(1)} %add_rsqrt_fusion.1) | copy-start | bytes 18916
  53.0 158.2 %reduce-scatter.16.cloned.1.call-start = ((), (), s32[]{:S(2)}) async-start(), calls=%async_computation.10 | async-start | bytes 4034560 | tf_op jit(solution)/shard_map/reduce_scatter | solution.py:130
  67.6 95.5 %copy-start.22 = (bf16[128,512]{0,1:T(8,128)(2,1)}, bf16[128,512]{0,1:T(8,128)(2,1)S(1)}, u32[]{:S(2)}) copy-start(bf16[128,512]{0,1:T(8,128)(2,1)S(1)} %all_gather.29) | copy-start | bytes 393220
  162.2 49.0 %copy-start.6 = (bf16[1576,128]{1,0:T(8,128)(2,1)S(1)}, bf16[1576,128]{1,0:T(8,128)(2,1)}, u32[]{:S(2)}) copy-start(bf16[1576,128]{1,0:T(8,128)(2,1)} %param.13) | copy-start | bytes 1210372
  162.2 68.9 %copy-start.43 = (f32[128]{0:T(128)S(1)}, f32[128]{0:T(128)}, u32[]{:S(2)}) copy-start(f32[128]{0:T(128)} %param.18) | copy-start | bytes 1540
  162.2 68.9 %copy-start.46 = (f32[128]{0:T(128)S(1)}, f32[128]{0:T(128)}, u32[]{:S(2)}) copy-start(f32[128]{0:T(128)} %param.19) | copy-start | bytes 1540
  163.1 71.0 %copy-start.26 = (s32[1576,2]{0,1:T(2,128)S(1)}, s32[1576,2]{0,1:T(2,128)}, u32[]{:S(2)}) copy-start(s32[1576,2]{0,1:T(2,128)} %param.23) | copy-start | bytes 37828
  165.4 69.8 %copy-start.20 = (bf16[1576,128]{1,0:T(8,128)(2,1)S(1)}, bf16[1576,128]{1,0:T(8,128)(2,1)}, u32[]{:S(2)}) copy-start(bf16[1576,128]{1,0:T(8,128)(2,1)} %param.25) | copy-start | bytes 1210372
  165.4 110.0 %all-reduce.5.cloned.1.call-start = ((), (), s32[]{:S(2)}) async-start(), calls=%async_computation.11 | async-start | bytes 425984 | tf_op jit(solution)/shard_map/psum | solution.py:134
  212.7 22.0 %copy-start.5 = (f32[1576,128]{1,0:T(8,128)}, f32[1576,128]{1,0:T(8,128)S(1)}, u32[]{:S(2)}) copy-start(f32[1576,128]{1,0:T(8,128)S(1)} %get-tuple-element.74) | copy-start | bytes 2420740
  221.8 12.1 copy-start.29
  231.7 92.5 %copy-start.1 = (bf16[1576,128]{1,0:T(8,128)(2,1)}, bf16[1576,128]{1,0:T(8,128)(2,1)S(1)}, u32[]{:S(2)}) copy-start(bf16[1576,128]{1,0:T(8,128)(2,1)S(1)} %add_convert_fusion.1) | copy-start | bytes 1210372
  232.7 153.8 %all-gather.7.cloned.1.call-start = ((), (), s32[]{:S(2)}) async-start(), calls=%async_computation.12 | async-start | bytes 18874368 | tf_op jit(solution)/shard_map/all_gather | solution.py:30
  233.2 303.8 %all-gather.9.cloned.1.call-start = ((), (), s32[]{:S(2)}) async-start(), calls=%async_computation.14 | async-start | bytes 18874368 | tf_op jit(solution)/shard_map/all_gather | solution.py:31
  233.8 354.0 %all-gather.11.cloned.1.call-start = ((), (), s32[]{:S(2)}) async-start(), calls=%async_computation.15 | async-start | bytes 4915200 | tf_op jit(solution)/shard_map/all_gather | solution.py:173
  262.5 15.9 copy-start.25
  303.1 284.8 %reduce-scatter.18.cloned.1.call-start = ((), (), s32[]{:S(2)}) async-start(), calls=%async_computation.13 | async-start | bytes 19660800 | tf_op jit(solution)/shard_map/reduce_scatter | solution.py:148
  324.2 75.5 %copy-start.27 = (bf16[32,120]{1,0:T(8,128)(2,1)}, bf16[32,120]{1,0:T(8,128)(2,1)S(1)}, u32[]{:S(2)}) copy-start(bf16[32,120]{1,0:T(8,128)(2,1)S(1)} %convert_element_type.92) | copy-start | bytes 23044
  331.6 68.0 %copy-start.8 = (bf16[3840,128]{1,0:T(8,128)(2,1)}, bf16[3840,128]{1,0:T(8,128)(2,1)S(1)}, u32[]{:S(2)}) copy-start(bf16[3840,128]{1,0:T(8,128)(2,1)S(1)} %gather_fusion) | copy-start | bytes 2949124
  399.7 415.9 %reduce-scatter.28.cloned.1.call-start = ((), (), s32[]{:S(2)}) async-start(), calls=%async_computation.23 | async-start | bytes 4915200
  643.0 215.5 %all-gather.13.cloned.1.call-start = ((), (), s32[]{:S(2)}) async-start(), calls=%async_computation.16 | async-start | bytes 19660800 | tf_op jit(solution)/shard_map/all_gather | solution.py:181
  643.7 298.7 %all-gather.15.cloned.1.call-start = ((), (), s32[]{:S(2)}) async-start(), calls=%async_computation.17 | async-start | bytes 2017280 | tf_op jit(solution)/shard_map/all_gather | solution.py:200
  822.5 35.8 %copy-start.11 = (f32[1576,32]{0,1:T(8,128)S(1)}, f32[1576,32]{0,1:T(8,128)}, u32[]{:S(2)}) copy-start(f32[1576,32]{0,1:T(8,128)} %all-reduce.5.cloned.1.call-done) | copy-start | bytes 605188
  871.1 16.8 copy-start.30
  871.1 16.8 copy-start.36
  878.1 33.1 %copy-start.34 = (f32[8,2,197]{2,1,0:T(2,128)S(1)}, f32[8,2,197]{2,1,0:T(2,128)}, u32[]{:S(2)}) copy-start(f32[8,2,197]{2,1,0:T(2,128)} %copy-done.33) | copy-start | bytes 37828
  878.1 64.3 %copy-start.23 = (bf16[128,512]{0,1:T(8,128)(2,1)S(1)}, bf16[128,512]{0,1:T(8,128)(2,1)}, u32[]{:S(2)}) copy-start(bf16[128,512]{0,1:T(8,128)(2,1)} %copy-done.22) | copy-start | bytes 393220
  878.1 72.8 %copy-start.4 = (f32[8,2,197,197]{2,3,1,0:T(8,128)S(1)}, f32[8,2,197,197]{2,3,1,0:T(8,128)}, u32[]{:S(2)}) copy-start(f32[8,2,197,197]{2,3,1,0:T(8,128)} %copy-done.3) | copy-start | bytes 7451332
  911.0 113.8 %all-gather.17.cloned.1.call-start = ((), (), s32[]{:S(2)}) async-start(), calls=%async_computation.18 | async-start | bytes 6389760 | tf_op jit(solution)/shard_map/all_gather | solution.py:235
  956.0 68.8 %copy-start.7 = (bf16[1576,128]{1,0:T(8,128)(2,1)S(1)}, bf16[1576,128]{1,0:T(8,128)(2,1)}, u32[]{:S(2)}) copy-start(bf16[1576,128]{1,0:T(8,128)(2,1)} %param.13) | copy-start | bytes 1210372
  956.0 68.8 %copy-start.32 = (f32[1576]{0:T(1024)S(1)}, f32[1576]{0:T(1024)}, u32[]{:S(2)}) copy-start(f32[1576]{0:T(1024)} %copy-done.31) | copy-start | bytes 18916
  956.0 68.8 %copy-start.38 = (f32[1576]{0:T(1024)S(1)}, f32[1576]{0:T(1024)}, u32[]{:S(2)}) copy-start(f32[1576]{0:T(1024)} %copy-done.37) | copy-start | bytes 18916
  956.0 68.8 %copy-start.41 = (f32[128]{0:T(128)S(1)}, f32[128]{0:T(128)}, u32[]{:S(2)}) copy-start(f32[128]{0:T(128)} %param.14) | copy-start | bytes 1540
  960.5 70.0 %copy-start.44 = (f32[128]{0:T(128)S(1)}, f32[128]{0:T(128)}, u32[]{:S(2)}) copy-start(f32[128]{0:T(128)} %get-tuple-element.55) | copy-start | bytes 1540
  960.5 70.0 %copy-start.45 = (f32[128]{0:T(128)S(1)}, f32[128]{0:T(128)}, u32[]{:S(2)}) copy-start(f32[128]{0:T(128)} %get-tuple-element.63) | copy-start | bytes 1540
  960.5 70.8 %copy-start.10 = (bf16[1576,512]{1,0:T(8,128)(2,1)S(1)}, bf16[1576,512]{1,0:T(8,128)(2,1)}, u32[]{:S(2)}) copy-start(bf16[1576,512]{1,0:T(8,128)(2,1)} %all-gather.15.cloned.1.call-done) | copy-start | bytes 4841476
  960.5 70.8 %copy-start.17 = (bf16[1576,128]{0,1:T(8,128)(2,1)S(1)}, bf16[1576,128]{0,1:T(8,128)(2,1)}, u32[]{:S(2)}) copy-start(bf16[1576,128]{0,1:T(8,128)(2,1)} %copy-done.16) | copy-start | bytes 1210372
  964.3 68.8 %copy-start.42 = (f32[128]{0:T(128)S(1)}, f32[128]{0:T(128)}, u32[]{:S(2)}) copy-start(f32[128]{0:T(128)} %param.15) | copy-start | bytes 1540
  964.3 126.6 %reduce-scatter.30.cloned.1.call-start = ((), (), s32[]{:S(2)}) async-start(), calls=%async_computation.24 | async-start | bytes 73728
  1031.2 64.2 %reduce-scatter.22.cloned.1.call-start = ((), (), s32[]{:S(2)}) async-start(), calls=%async_computation.20 | async-start | bytes 294912 | tf_op jit(solution)/shard_map/reduce_scatter | solution.py:248
  1032.8 92.3 %reduce-scatter.20.cloned.1.call-start = ((), (), s32[]{:S(2)}) async-start(), calls=%async_computation.19 | async-start | bytes 884736 | tf_op jit(solution)/shard_map/reduce_scatter | solution.py:247
  1038.1 413.5 %reduce-scatter.26.cloned.1.call-start = ((), (), s32[]{:S(2)}) async-start(), calls=%async_computation.22 | async-start | bytes 37748736 | tf_op jit(solution)/shard_map/reduce_scatter | solution.py:190
  1055.5 722.9 %reduce-scatter.24.cloned.1.call-start = ((), (), s32[]{:S(2)}) async-start(), calls=%async_computation.21 | async-start | bytes 37748736 | tf_op jit(solution)/shard_map/reduce_scatter | solution.py:189
  1073.6 15.3 copy-start.18
  1073.6 15.3 copy-start.24
  (15 other events, 35.2 us)
Sparse Core Ops, SparseCore 0:
  53.1 101.3 reduce-scatter.13
  165.5 45.6 reduce-scatter.15
  232.8 42.6 all-reduce.4
  399.8 144.7 reduce-scatter.17
  643.1 172.4 reduce-scatter.27
  911.1 31.1 all-gather.14
  964.4 60.3 all-gather.16
Sparse Core Ops, SparseCore 1:
  234.7 151.6 all-gather.6
  387.9 149.1 all-gather.8
  539.5 48.4 all-gather.10
  646.3 157.7 all-gather.12
  1031.3 29.9 reduce-scatter.29
  1064.1 28.5 reduce-scatter.21
  1095.5 29.6 reduce-scatter.19
  1127.9 323.6 reduce-scatter.25
  1454.5 323.8 reduce-scatter.23
where the time goes:
time: 1790 us
  waiting for transfers between devices  1330 us (74%)
  local copies, waits for them, and re-layouts  137 us (8%)
  matrix products  133 us (7%)
  blocking collectives  113 us (6%)
  other arithmetic  56.8 us (3%)
    reduce_scatter x1, waiting for transfers between devices, local(): lax.psum_scatter(in_expert_grad, 'col', scatter_dimension=2, tiled=True)  327 us
    reduce_scatter x1, waiting for transfers between devices, local(): lax.psum_scatter(out_expert_grad, 'col', scatter_dimension=2, tiled=True)  326 us
    unnamed x18, waiting for transfers between devices  172 us
    all_gather x1, waiting for transfers between devices, expert_weights(): lax.all_gather(expert_out, 'col', axis=2, tiled=True)  137 us
    reduce_scatter x1, waiting for transfers between devices, local(): lax.psum_scatter(partial_qkv, 'row', scatter_dimension=2, tiled=True)  86.9 us
    psum x7, blocking collectives, row_totals(): return lax.psum(pieces, 'row')  83.8 us
    all_gather x1, waiting for transfers between devices, local(): lax.all_gather(grad_project, 'row', axis=2, tiled=True)  60.2 us
    all_gather x1, waiting for transfers between devices, expert_weights(): lax.all_gather(expert_in, 'col', axis=2, tiled=True)  54.8 us
  transfers between devices with their start and end apart: 16, of which 12 were waited for; matrix products, arithmetic and copies ran while one was open for 10% of the time, Pallas kernels for 0%

commit v1 on v0

v1 whole, which is shorter than its diff:
```python
from functools import partial

import jax
import jax.numpy as jnp
from jax import lax
from jax.sharding import PartitionSpec as P

E = 32
SEQ = 197
HD = 64
CAP = 120
EPS_NORM = 1e-06
F32 = jnp.float32
BF16 = jnp.bfloat16


def dot(a, b, dims):
    return lax.dot_general(a, b, (dims, ((), ())), preferred_element_type=F32)


def col_groups():
    rows, cols = lax.axis_size("row"), lax.axis_size("col")
    near = E // rows
    return cols // near, near


def exchange(pieces):
    groups, near = col_groups()
    if groups == 1:
        return lax.all_to_all(pieces, ("row", "col"), 0, 0, tiled=True)
    rows = lax.axis_size("row")
    index = [[g * near + c for c in range(near)] for g in range(groups)]
    parts = pieces.reshape((rows, near) + pieces.shape[1:])
    parts = lax.all_to_all(parts, "row", 0, 0, tiled=True)
    parts = lax.all_to_all(parts, "col", 1, 1, tiled=True, axis_index_groups=index)
    return parts.reshape(pieces.shape)


def far_groups():
    groups, near = col_groups()
    return [[g * near + c for g in range(groups)] for c in range(near)]


def collect_far(x):
    if col_groups()[0] == 1:
        return x[None]
    return lax.all_gather(x, "col", axis=0, axis_index_groups=far_groups())


def reduce_far(x):
    if col_groups()[0] == 1:
        return x[0]
    return lax.psum_scatter(x, "col", scatter_dimension=0, axis_index_groups=far_groups())


def spread(x, axis, groups=None):
    n = len(groups[0]) if groups else lax.axis_size(axis)
    return lax.all_to_all(
        jnp.broadcast_to(x[None], (n,) + x.shape), axis, 0, 0, tiled=True, axis_index_groups=groups
    )


def gather_all(x):
    half = lax.axis_size("col") // 2
    far = spread(x, "col", [[2 * i + k for i in range(half)] for k in range(2)])
    mine = spread(far, "row")
    swap = [(i, i ^ 1) for i in range(2 * half)]
    other = lax.ppermute(mine, "col", swap)
    first = lax.axis_index("col") % 2 == 0
    both = jnp.stack([jnp.where(first, mine, other), jnp.where(first, other, mine)], axis=2)
    return both.reshape((both.shape[0], 2 * half) + x.shape)


def to_tokens(x):
    rows = lax.axis_size("row")
    t, w = x.shape
    y = lax.all_to_all(x.reshape(rows, t // rows, w), "row", 0, 0, tiled=True)
    return y.transpose(1, 0, 2).reshape(t // rows, rows * w)


def to_features(x):
    rows = lax.axis_size("row")
    t, w = x.shape
    y = x.reshape(t, rows, w // rows).transpose(1, 0, 2)
    return lax.all_to_all(y, "row", 0, 0, tiled=True).reshape(t * rows, w // rows)


def normalize(values):
    average = jnp.mean(values, axis=1, keepdims=True)
    centred = values - average
    inverse = lax.rsqrt(jnp.mean(centred * centred, axis=1, keepdims=True) + EPS_NORM)
    return centred * inverse, inverse


def norm_backward(grad_normed, normalized, inverse, gain):
    scaled = grad_normed * gain
    plain = jnp.mean(scaled, axis=1, keepdims=True)
    cross = jnp.mean(scaled * normalized, axis=1, keepdims=True)
    return inverse * (scaled - plain - normalized * cross)


def softmax_last(scores):
    top_value = jnp.max(scores, axis=-1, keepdims=True)
    powers = jnp.exp(scores - top_value)
    return powers / jnp.sum(powers, axis=-1, keepdims=True)


def slot_table(routes, keep):
    t = routes.shape[0]
    experts = jnp.arange(E, dtype=jnp.int32)
    onehot = routes[:, :, None] == experts[None, None, :]
    named = jnp.any(onehot, axis=1).astype(BF16)
    steps = jnp.arange(t, dtype=jnp.int32)
    earlier = (steps[None, :] < steps[:, None]).astype(BF16)
    counts = dot(earlier, named, ((1,), (0,))).astype(jnp.int32)
    place = jnp.sum(jnp.where(onehot, counts[:, None, :], 0), axis=2)
    return jnp.where(keep != 0, routes * CAP + place, -1)


def local(
    tokens,
    ln1_gain,
    ln1_bias,
    qkv_weight,
    out_weight,
    ln2_gain,
    ln2_bias,
    router_weight,
    expert_in,
    expert_out,
    routes,
    keep,
    cotangent,
):
    rows, cols = lax.axis_size("row"), lax.axis_size("col")
    groups, near = col_groups()
    block_tok, width_part = tokens.shape
    width = width_part * rows
    heads = width // HD
    mine = block_tok // rows
    images = mine // SEQ
    hid_part = expert_in.shape[2]
    hid = hid_part * cols
    out_part = expert_out.shape[2]
    qkv_part, mix_part = qkv_weight.shape[1], out_weight.shape[1]
    score_scale = HD ** (-0.5)

    slots = slot_table(routes, keep)
    hits = jnp.any(
        slots[:, :, None] == jnp.arange(E * CAP, dtype=jnp.int32)[None, None, :], axis=1
    ).astype(BF16)

    small = gather_all(jnp.concatenate([qkv_weight.T, out_weight.T], axis=0))
    qkv_t = small[:, :, :qkv_part].transpose(1, 2, 0, 3).reshape(3 * width, width)
    mix_t = small[:, :, qkv_part:].transpose(1, 2, 0, 3).reshape(width, width)
    norms = spread(jnp.stack([ln1_gain, ln1_bias, ln2_gain, ln2_bias]), "row")
    norms = norms.transpose(1, 0, 2).reshape(4, width)
    router_t = spread(router_weight.T, "row").transpose(1, 0, 2).reshape(E, width)
    w_in = exchange(expert_in).reshape(rows, near, width_part, hid_part)
    w_in = collect_far(w_in).transpose(1, 3, 0, 2, 4).reshape(width, hid)
    w_out_t = exchange(expert_out.transpose(0, 2, 1)).reshape(rows, near, out_part, hid // rows)
    w_out_t = collect_far(w_out_t).transpose(0, 2, 3, 1, 4).reshape(width, hid)

    def dispatch(values):
        picked = dot(hits, values, ((0,), (0,))).astype(BF16)
        got = exchange(picked.reshape(E, CAP, width_part))
        got = got.reshape(rows, near, CAP, width_part).transpose(1, 2, 0, 3)
        return got.reshape(near * CAP, width)

    def combine(values):
        sent = values.astype(BF16).reshape(near, CAP, rows, width_part).transpose(2, 0, 1, 3)
        got = exchange(sent.reshape(E, CAP, width_part))
        return dot(hits, got.reshape(E * CAP, width_part), ((1,), (0,)))

    cot_rows = dispatch(cotangent).astype(F32)
    tok_float = to_tokens(tokens).astype(F32)
    grad_out = to_tokens(cotangent).astype(F32)

    normal1, inverse1 = normalize(tok_float)
    normed1 = (normal1 * norms[0] + norms[1]).astype(BF16)
    project = dot(normed1, qkv_t, ((1,), (1,))).astype(BF16)
    split_heads = project.reshape(images, SEQ, 3, heads, HD)
    queries, keys_all, values_all = (split_heads[:, :, i] for i in range(3))
    scores = score_scale * jnp.einsum(
        "bqhd,bkhd->bhqk", queries, keys_all, preferred_element_type=F32
    )
    float_probs = softmax_last(scores)
    attn_probs = float_probs.astype(BF16)
    attended = jnp.einsum("bhqk,bkhd->bqhd", attn_probs, values_all, preferred_element_type=F32)
    attended = attended.reshape(mine, width).astype(BF16)
    attn_out = dot(attended, mix_t, ((1,), (1,)))
    residual = tok_float + attn_out
    normal2, inverse2 = normalize(residual)
    normed2 = (normal2 * norms[2] + norms[3]).astype(BF16)
    attn_part = to_features(attn_out.astype(BF16))

    x_rows = dispatch(to_features(normed2))
    flat = lax.axis_index("row") * near + lax.axis_index("col") % near
    gates = softmax_last(dot(x_rows, router_t, ((1,), (1,))))
    own = (jnp.arange(E) == flat).astype(F32)[None, :]
    chosen = jnp.sum(gates * own, axis=1, keepdims=True)
    pre_act = dot(x_rows, w_in, ((1,), (0,)))
    activated, gelu_back = jax.vjp(partial(jax.nn.gelu, approximate=False), pre_act)
    activated = activated.astype(BF16)
    expert_res = dot(activated, w_out_t, ((1,), (1,)))
    grad_chosen = jnp.sum(cot_rows * expert_res, axis=1, keepdims=True)
    grad_logits = (grad_chosen * chosen * (own - gates)).astype(BF16)
    grad_res = (chosen * cot_rows).astype(BF16)
    grad_act = dot(grad_res, w_out_t, ((1,), (0,)))
    (grad_pre,) = gelu_back(grad_act)
    grad_pre = grad_pre.astype(BF16)
    grad_rows = dot(grad_pre, w_in, ((1,), (1,))) + dot(grad_logits, router_t, ((1,), (0,)))
    grad_norm2 = to_tokens(combine(grad_rows).astype(BF16)).astype(F32)
    moved = combine(chosen * expert_res)
    layer_out = (tokens.astype(F32) + attn_part.astype(F32) + moved).astype(BF16)
    router_part = dot(grad_logits, x_rows, ((0,), (0,)))
    out_grad_t = dot(grad_res, activated, ((0,), (0,))).astype(BF16)
    in_grad = dot(x_rows, grad_pre, ((0,), (0,))).astype(BF16)
    out_grad_t = out_grad_t.reshape(groups, near, out_part, rows, hid // rows).transpose(0, 3, 1, 2, 4)
    out_grad_t = exchange(reduce_far(out_grad_t).reshape(E, out_part, hid // rows))
    in_grad = in_grad.reshape(rows, width_part, groups, near, hid_part).transpose(2, 0, 3, 1, 4)
    in_grad = exchange(reduce_far(in_grad).reshape(E, width_part, hid_part))
    expert_out_grad = out_grad_t.astype(F32).transpose(0, 2, 1)
    expert_in_grad = in_grad.astype(F32)

    gain2_part = jnp.sum(grad_norm2 * normal2, axis=0)
    bias2_part = jnp.sum(grad_norm2, axis=0)
    grad_resid = grad_out + norm_backward(grad_norm2, normal2, inverse2, norms[2])
    grad_attn = grad_resid.astype(BF16)
    mix_grad_t = dot(grad_attn, attended, ((0,), (0,)))
    grad_heads = dot(grad_attn, mix_t, ((1,), (0,))).astype(BF16).reshape(images, SEQ, heads, HD)
    grad_values = jnp.einsum(
        "bhqk,bqhd->bkhd", attn_probs, grad_heads, preferred_element_type=F32
    )
    grad_probs = jnp.einsum("bqhd,bkhd->bhqk", grad_heads, values_all, preferred_element_type=F32)
    row_dot = jnp.sum(float_probs * grad_probs, axis=-1, keepdims=True)
    grad_scores = (float_probs * (grad_probs - row_dot)).astype(BF16)
    grad_queries = score_scale * jnp.einsum(
        "bhqk,bkhd->bqhd", grad_scores, keys_all, preferred_element_type=F32
    )
    grad_keys = score_scale * jnp.einsum(
        "bhqk,bqhd->bkhd", grad_scores, queries, preferred_element_type=F32
    )
    grad_project = jnp.stack([grad_queries, grad_keys, grad_values], axis=2)
    grad_project = grad_project.reshape(mine, 3 * width).astype(BF16)
    qkv_grad_t = dot(grad_project, normed1, ((0,), (0,)))
    grad_norm1 = dot(grad_project, qkv_t, ((1,), (0,)))
    gain1_part = jnp.sum(grad_norm1 * normal1, axis=0)
    bias1_part = jnp.sum(grad_norm1, axis=0)
    tokens_grad = grad_resid + norm_backward(grad_norm1, normal1, inverse1, norms[0])
    tokens_grad = to_features(tokens_grad.astype(BF16)).astype(F32)

    shares = jnp.concatenate(
        [
            qkv_grad_t.reshape(cols, qkv_part, width),
            mix_grad_t.reshape(cols, mix_part, width),
            jnp.broadcast_to(router_part[None], (cols, E, width)),
            jnp.broadcast_to(
                jnp.stack([gain1_part, bias1_part, gain2_part, bias2_part])[None], (cols, 4, width)
            ),
        ],
        axis=1,
    ).astype(BF16)
    depth = shares.shape[1]
    shares = shares.reshape(cols, depth, rows, width_part).transpose(2, 0, 1, 3)
    shares = shares.reshape(rows * cols, depth, width_part)
    shares = lax.all_to_all(shares, ("row", "col"), 0, 0, tiled=True)
    sums = jnp.sum(shares.astype(F32), axis=0)
    thin = width_part // cols
    tail = lax.dynamic_slice_in_dim(
        sums[qkv_part + mix_part :], lax.axis_index("col") * thin, thin, axis=1
    )
    return (
        layer_out,
        tokens_grad,
        tail[E],
        tail[E + 1],
        sums[:qkv_part].T,
        sums[qkv_part : qkv_part + mix_part].T,
        tail[E + 2],
        tail[E + 3],
        tail[:E].T,
        expert_in_grad,
        expert_out_grad,
    )


def solution(mesh):
    in_specs = (
        P("col", "row"),
        P("row"),
        P("row"),
        P("row", "col"),
        P("row", "col"),
        P("row"),
        P("row"),
        P("row", None),
        P(None, "row", "col"),
        P(None, "row", "col"),
        P("col", None),
        P("col", None),
        P("col", "row"),
    )
    out_specs = (
        P("col", "row"),
        P("col", "row"),
        P(("row", "col")),
        P(("row", "col")),
        P("row", "col"),
        P("row", "col"),
        P(("row", "col")),
        P(("row", "col")),
        P(("row", "col"), None),
        P(None, "row", "col"),
        P(None, "row", "col"),
    )
    return jax.shard_map(local, mesh=mesh, in_specs=in_specs, out_specs=out_specs, check_vma=False)
```

time: 1790 us -> 584 us (0.33)
  waiting for transfers between devices: 1330 us -> 218 us
  starting transfers between devices: 1.7 us -> 65.8 us
  local copies, waits for them, and re-layouts: 137 us -> 81.1 us
  blocking collectives: 113 us -> 65.7 us
  matrix products: 133 us -> 104 us
    reduce_scatter x7 -> x0, waiting for transfers between devices: 816 us -> none  [the longest x1 327 us: local(): lax.psum_scatter(in_expert_grad, 'col', scatter_dimension=2, tiled=True)]
    all_gather x6 -> x0, waiting for transfers between devices: 333 us -> none  [the longest x1 137 us: expert_weights(): lax.all_gather(expert_out, 'col', axis=2, tiled=True)]
    all_to_all x0 -> x17, waiting for transfers between devices: none -> 218 us  [the longest x7 169 us: exchange(): return lax.all_to_all(pieces, ('row', 'col'), 0, 0, tiled=True)]
    unnamed x18 -> x0, waiting for transfers between devices: 172 us -> none
    psum x7 -> x0, blocking collectives: 83.8 us -> none  [row_totals(): return lax.psum(pieces, 'row')]
    gather x6 -> x0, local copies, waits for them, and re-layouts: 68 us -> none  [the longest x1 20.2 us: slot_tables(): slot_keep = keep_ext[pair_of_slot]]
    all_to_all x0 -> x17, starting transfers between devices: none -> 65.7 us  [the longest x7 25 us: exchange(): return lax.all_to_all(pieces, ('row', 'col'), 0, 0, tiled=True)]
    all_to_all x0 -> x2, blocking collectives: none -> 65.7 us  [the longest x1 53.9 us: exchange(): return lax.all_to_all(pieces, ('row', 'col'), 0, 0, tiled=True)]
  transfers between devices with their start and end apart: 16 -> 18, of which waited for: 12 -> 10; matrix products, arithmetic and copies ran while one was open for 10% -> 33% of each run, Pallas kernels for 0% -> 0%
where the time goes in v1:
time: 584 us; the launch traced here: 577 us
  waiting for transfers between devices  218 us (37%)
  matrix products  104 us (18%)
  local copies, waits for them, and re-layouts  81.1 us (14%)
  starting transfers between devices  65.8 us (11%)
  blocking collectives  65.7 us (11%)
  other arithmetic  40.1 us (7%)
    all_to_all x7, waiting for transfers between devices, exchange(): return lax.all_to_all(pieces, ('row', 'col'), 0, 0, tiled=True)  169 us
    dot_general x20, matrix products, dot(): return lax.dot_general(a, b, (dims, ((), ())), preferred_element_type=F32)  97.1 us
    all_to_all x1, blocking collectives, exchange(): return lax.all_to_all(pieces, ('row', 'col'), 0, 0, tiled=True)  53.9 us
    all_to_all x1, waiting for transfers between devices, local(): shares = lax.all_to_all(shares, ('row', 'col'), 0, 0, tiled=True)  38.6 us
    all_to_all x7, starting transfers between devices, exchange(): return lax.all_to_all(pieces, ('row', 'col'), 0, 0, tiled=True)  25 us
    unnamed x153, local copies, waits for them, and re-layouts  21.3 us
    all_to_all x4, starting transfers between devices, spread(): lax.all_to_all(jnp.broadcast_to(x[None], (n,) + x.shape), axis, 0, 0, til...  17.2 us
    reduce_or x1, other arithmetic, local(): jnp.any(slots[:, :, None] == jnp.arange(E * CAP, dtype=jnp.int32)[None, N...  17.1 us
  transfers between devices with their start and end apart: 18, of which 10 were waited for; matrix products, arithmetic and copies ran while one was open for 33% of the time, Pallas kernels for 0%

profile of v1, /device:TPU:0, one launch (start us, length us, event | category | flops | bytes accessed | tf_op | source)
XLA Modules:
  0.0 576.6 jit_solution(14911296433307233857)
XLA Ops:
  2.0 5.2 all-to-all-start.1
  8.0 3.9 all-to-all-done.1
  12.6 4.9 all-to-all-start.2
  19.4 5.0 all-to-all-done.2
  25.6 3.5 all-to-all-start.3
  30.0 17.1 %fusion.1 = pred[1576,3840]{1,0:T(8,128)(4,1)} fusion(s32[1576,2]{0,1:T(2,128)S(1)} %compare_select_fusion), kind=kLoop, calls=%fused_computation.2 | loop fusion | flops 18155520 | bytes 6064448 | tf_op jit(solution)/shard_map/reduce_or | solution.py:149
  47.0 4.7 all-to-all-start
  51.7 10.5 %convolution_convert_fusion = bf16[3840,128]{1,0:T(8,128)(2,1)} fusion(pred[1576,3840]{1,0:T(8,128)(4,1)} %fusion.1, bf16[1576,128]{1,0:T(8,128)(2,1)S(1)} %copy-done.33), kind=kOutput, calls=%fused_computation.22 | convolution fusion | flops 1549762560 | bytes 7438336 | tf_op jit(solution)/shard_map/dot_general | solution.py:18
  62.4 5.0 all-to-all-start.12
  76.4 3.1 reshape.340
  86.9 2.8 fusion.80
  97.8 11.8 %all_to_all.95 = bf16[4,394,128]{2,1,0:T(8,128)(2,1)S(1)} all-to-all(bf16[4,394,128]{2,1,0:T(8,128)(2,1)S(1)} %bitcast.323), channel_id=1, replica_groups=mesh['row'=4,'col'=8] {'row'}, dimensions={0} | all-to-all | bytes 806912 | tf_op jit(solution)/shard_map/all_to_all | solution.py:85
  109.5 53.9 %all_to_all.96 = bf16[32,128,256]{2,1,0:T(8,128)(2,1)} all-to-all(bf16[32,128,256]{2,1,0:T(8,128)(2,1)} %param.21), channel_id=1, replica_groups=mesh['row'=4,'col'=8] {'row','col'}, dimensions={0} | all-to-all | bytes 4194304 | tf_op jit(solution)/shard_map/all_to_all | solution.py:30
  163.5 3.7 all-to-all-start.9
  167.3 10.5 %convolution_convert_fusion.1 = bf16[3840,128]{1,0:T(8,128)(2,1)} fusion(pred[1576,3840]{1,0:T(8,128)(4,1)} %fusion.1, bf16[1576,128]{1,0:T(8,128)(2,1)S(1)} %reshape.306), kind=kOutput, calls=%fused_computation.23 | convolution fusion | flops 1549762560 | bytes 7438336 | tf_op jit(solution)/shard_map/dot_general | solution.py:18
  177.8 39.4 %all-to-all-done.9 = bf16[32,64,512]{2,1,0:T(8,128)(2,1)} async-done(((bf16[32,64,512]{2,1,0:T(8,128)(2,1)}), bf16[32,64,512]{2,1,0:T(8,128)(2,1)}, u32[]{:S(2)}, u32[]{:S(2)}) %all-to-all-start.9) | async-done | bytes 2097184 | tf_op jit(solution)/shard_map/all_to_all | solution.py:30
  217.3 2.6 all-to-all-start.6
  220.1 2.6 copy.236
  225.9 3.2 copy.232
  231.1 15.0 %all-to-all-done.6 = bf16[32,120,128]{2,1,0:T(8,128)(2,1)S(1)} async-done(((bf16[32,120,128]{2,1,0:T(8,128)(2,1)}), bf16[32,120,128]{2,1,0:T(8,128)(2,1)S(1)}, u32[]{:S(2)}, u32[]{:S(2)}) %all-to-all-start.6) | async-done | bytes 983072 | tf_op jit(solution)/shard_map/all_to_all | solution.py:30
  246.7 3.7 all-to-all-start.7
  252.1 21.9 %multiply_convert_fusion = (bf16[960,2048]{1,0:T(8,128)(2,1)}, f32[960,2048]{1,0:T(8,128)}, f32[960,2048]{1,0:T(8,128)}) fusion(bf16[512,2048]{1,0:T(8,128)(2,1)} %bitcast.316, bf16[120,8,4,128]{3,2,1,0:T(4,128)(2,1)S(1)} %bitcast.328), kind=kOutput, calls=%fused_computation.8 | convolution fusion | flops 2141061120 | bytes 22740992 | tf_op jit(solution)/shard_map/dot_general | solution.py:18
  278.1 8.1 %add_convert_fusion = bf16[960,2048]{1,0:T(8,128)(2,1)S(1)} fusion(f32[960,2048]{1,0:T(8,128)} %get-tuple-element.88, f32[960,2048]{1,0:T(8,128)} %get-tuple-element.110, bf16[512,2048]{1,0:T(8,128)(2,1)S(1)} %bitcast.314, bf16[120,8,4,128]{3,2,1,0:T(4,128)(2,1)S(1)} %bitcast.335), kind=kOutput, calls=%fused_computation.7 | convolution fusion | flops 2040791040 | bytes 22740992 | tf_op jit(solution)/shard_map/dot_general | solution.py:18
  290.3 3.2 fusion.15
  295.5 3.3 all-to-all-start.13
  299.6 25.3 %all-to-all-done.13 = bf16[32,120,128]{2,1,0:T(8,128)(2,1)S(1)} async-done(((bf16[32,120,128]{2,1,0:T(8,128)(2,1)}), bf16[32,120,128]{2,1,0:T(8,128)(2,1)S(1)}, u32[]{:S(2)}, u32[]{:S(2)}) %all-to-all-start.13) | async-done | bytes 983072 | tf_op jit(solution)/shard_map/all_to_all | solution.py:30
  324.9 3.5 all-to-all-start.11
  328.4 6.0 %convolution_convert_fusion.5 = bf16[1576,128]{1,0:T(8,128)(2,1)S(1)} fusion(pred[1576,3840]{1,0:T(8,128)(4,1)} %fusion.1, bf16[3840,128]{1,0:T(8,128)(2,1)S(1)} %bitcast.334), kind=kOutput, calls=%fused_computation.38 | convolution fusion | flops 1549472768 | bytes 7438336 | tf_op jit(solution)/shard_map/dot_general | solution.py:18
  335.3 4.2 all-to-all-start.14
  345.8 4.3 all-to-all-start.4
  364.0 3.4 all-to-all-start.10
  367.8 2.6 convolution_bitcast_fusion
  374.7 3.7 multiply_reduce_fusion.3
  379.7 13.9 %all-to-all-done.10 = bf16[32,120,128]{2,1,0:T(8,128)(2,1)} async-done(((bf16[32,120,128]{2,1,0:T(8,128)(2,1)}), bf16[32,120,128]{2,1,0:T(8,128)(2,1)}, u32[]{:S(2)}, u32[]{:S(2)}) %all-to-all-start.10) | async-done | bytes 983072 | tf_op jit(solution)/shard_map/all_to_all | solution.py:30
  393.5 3.7 all-to-all-start.15
  397.3 4.5 convolution_convert_fusion.3
  405.1 3.3 all-to-all-start.17
  408.3 6.6 %convolution_convert_fusion.2 = bf16[512,2048]{1,0:T(8,128)(2,1)} fusion(bf16[960,2048]{1,0:T(8,128)(2,1)} %get-tuple-element.87, f32[120,8,4,128]{3,2,1,0:T(4,128)} %bitcast.319, f32[960]{0:T(1024)S(1)} %copy-done.50), kind=kOutput, calls=%fused_computation.30 | convolution fusion | flops 2015297536 | bytes 7999232 | tf_op jit(solution)/shard_map/dot_general | solution.py:18
  414.9 4.5 reshape.326
  419.4 3.5 copy.256
  422.9 35.5 %all-to-all-done.17 = bf16[32,128,256]{2,1,0:T(8,128)(2,1)S(1)} async-done(((bf16[32,128,256]{2,1,0:T(8,128)(2,1)}), bf16[32,128,256]{2,1,0:T(8,128)(2,1)S(1)}, u32[]{:S(2)}, u32[]{:S(2)}) %all-to-all-start.17) | async-done | bytes 2097184 | tf_op jit(solution)/shard_map/all_to_all | solution.py:30
  458.4 3.7 all-to-all-start.18
  472.8 39.5 %all-to-all-done.18 = bf16[32,64,512]{2,1,0:T(8,128)(2,1)} async-done(((bf16[32,64,512]{2,1,0:T(8,128)(2,1)}), bf16[32,64,512]{2,1,0:T(8,128)(2,1)}, u32[]{:S(2)}, u32[]{:S(2)}) %all-to-all-start.18) | async-done | bytes 2097184 | tf_op jit(solution)/shard_map/all_to_all | solution.py:30
  512.2 3.2 all-to-all-start.16
  517.5 7.3 %fusion.12 = bf16[1576,128]{1,0:T(8,128)(2,1)} fusion(pred[1576,3840]{1,0:T(8,128)(4,1)} %fusion.1, bf16[3840,128]{1,0:T(8,128)(2,1)} %bitcast.37, f32[1576,128]{1,0:T(8,128)} %reshape.327, bf16[1576,128]{1,0:T(8,128)(2,1)S(1)} %copy-done.36), kind=kOutput, calls=%fused_computation.41 | convolution fusion | flops 1550077952 | bytes 8648704 | tf_op jit(solution)/shard_map/dot_general | solution.py:18
  525.7 4.1 convert_element_type.243
  529.8 4.2 convert_bitcast_fusion
  534.0 38.6 %all-to-all-done.16 = bf16[32,292,128]{2,1,0:T(8,128)(2,1)S(1)} async-done(((bf16[32,292,128]{2,1,0:T(8,128)(2,1)}), bf16[32,292,128]{2,1,0:T(8,128)(2,1)S(1)}, u32[]{:S(2)}, u32[]{:S(2)}) %all-to-all-start.16) | async-done | bytes 2392096 | tf_op jit(solution)/shard_map/all_to_all | solution.py:267
  (267 shorter events, 97.0 us)
Async XLA Ops:
  0.6 18.6 %copy-start.39 = (s32[1576,2]{0,1:T(2,128)S(1)}, s32[1576,2]{0,1:T(2,128)}, u32[]{:S(2)}) copy-start(s32[1576,2]{0,1:T(2,128)} %param.23) | copy-start | bytes 37828
  2.0 9.9 %all-to-all-start.1 = ((f32[4,4,128]{2,1,0:T(4,128)}), f32[4,4,128]{2,1,0:T(4,128)S(1)}, u32[]{:S(2)}, u32[]{:S(2)}) async-start(f32[4,4,128]{2,1,0:T(4,128)} %broadcast_in_dim.28), calls=%async_computation.1 | async-start | bytes 16384 | tf_op jit(solution)/shard_map/all_to_all | solution.py:58
  12.6 11.8 %all-to-all-start.2 = ((bf16[4,256,128]{2,1,0:T(8,128)(2,1)}), bf16[4,256,128]{2,1,0:T(8,128)(2,1)S(1)}, u32[]{:S(2)}, u32[]{:S(2)}) async-start(bf16[4,256,128]{2,1,0:T(8,128)(2,1)} %broadcast_in_dim.29), calls=%async_computation.2 | async-start | bytes 524288 | tf_op jit(solution)/shard_map/all_to_all | solution.py:58
  18.2 10.9 %copy-start.62 = (s32[1576,2]{0,1:T(2,128)S(1)}, s32[1576,2]{0,1:T(2,128)}, u32[]{:S(2)}) copy-start(s32[1576,2]{0,1:T(2,128)} %param.24) | copy-start | bytes 37828
  18.2 10.9 %copy-start.35 = (bf16[1576,128]{1,0:T(8,128)(2,1)S(1)}, bf16[1576,128]{1,0:T(8,128)(2,1)}, u32[]{:S(2)}) copy-start(bf16[1576,128]{1,0:T(8,128)(2,1)} %param.13) | copy-start | bytes 1210372
  25.6 21.5 %all-to-all-start.3 = ((bf16[4,4,256,128]{3,2,1,0:T(8,128)(2,1)}), bf16[4,4,256,128]{3,2,1,0:T(8,128)(2,1)S(1)}, u32[]{:S(2)}, u32[]{:S(2)}) async-start(bf16[4,4,256,128]{3,2,1,0:T(8,128)(2,1)} %broadcast_in_dim.30), calls=%async_computation.3 | async-start | bytes 2097152 | tf_op jit(solution)/shard_map/all_to_all | solution.py:58
  29.1 22.6 %copy-start.33 = (bf16[1576,128]{1,0:T(8,128)(2,1)S(1)}, bf16[1576,128]{1,0:T(8,128)(2,1)}, u32[]{:S(2)}) copy-start(bf16[1576,128]{1,0:T(8,128)(2,1)} %param.25) | copy-start | bytes 1210372
  47.0 15.3 %all-to-all-start = ((bf16[4,394,128]{2,1,0:T(8,128)(2,1)}), bf16[4,394,128]{2,1,0:T(8,128)(2,1)S(1)}, u32[]{:S(2)}, u32[]{:S(2)}) async-start(bf16[4,394,128]{2,1,0:T(8,128)(2,1)} %reshape.299), calls=%async_computation | async-start | bytes 819200 | tf_op jit(solution)/shard_map/all_to_all | solution.py:77
  62.3 7.1 %copy-start.58 = (f32[1,4,128]{2,0,1:T(1,128)}, f32[1,4,128]{2,0,1:T(1,128)S(1)}, u32[]{:S(2)}) copy-start(f32[1,4,128]{2,0,1:T(1,128)S(1)} %get-tuple-element.106) | copy-start | bytes 6148
  62.3 33.4 %copy-start.40 = (f32[1,4,128]{2,0,1:T(1,128)}, f32[1,4,128]{2,0,1:T(1,128)S(1)}, u32[]{:S(2)}) copy-start(f32[1,4,128]{2,0,1:T(1,128)S(1)} %get-tuple-element.103) | copy-start | bytes 6148
  62.3 8.0 %collective-permute-start = (bf16[4,4,256,128]{3,2,1,0:T(8,128)(2,1)S(1)}, bf16[4,4,256,128]{3,2,1,0:T(8,128)(2,1)}, u32[]{:S(2)}, u32[]{:S(2)}) collective-permute-start(bf16[4,4,256,128]{3,2,1,0:T(8,128)(2,1)S(1)} %all-to-all-done.3), channel_id=1, source_target_pairs={{0,1},{1,0},{2,3},{3,2},{4,5},{5,4},{6,7},{7,6},{8,9},{9,8},{10,11... | collective-permute-start | bytes 3145736 | tf_op jit(solution)/shard_map/ppermute | solution.py:68
  62.4 35.4 %all-to-all-start.12 = ((bf16[32,120,128]{2,1,0:T(8,128)(2,1)}), bf16[32,120,128]{2,1,0:T(8,128)(2,1)S(1)}, u32[]{:S(2)}, u32[]{:S(2)}) async-start(bf16[32,120,128]{2,1,0:T(8,128)(2,1)} %bitcast.332), calls=%async_computation.12 | async-start | bytes 1966080 | tf_op jit(solution)/shard_map/all_to_all | solution.py:30
  82.7 7.1 %copy-start.31 = (bf16[2,197,1,8,64]{1,4,3,0,2:T(8,128)(2,1)}, bf16[2,197,1,8,64]{1,4,3,0,2:T(8,128)(2,1)S(1)}, u32[]{:S(2)}) copy-start(bf16[2,197,1,8,64]{1,4,3,0,2:T(8,128)(2,1)S(1)} %copy.270) | copy-start | bytes 1210372
  84.5 5.3 copy-start.12
  95.6 67.9 %copy-start.53 = (f32[394]{0:T(512)}, f32[394]{0:T(512)S(1)}, u32[]{:S(2)}) copy-start(f32[394]{0:T(512)S(1)} %add_rsqrt_fusion) | copy-start | bytes 4732
  163.5 53.8 %all-to-all-start.9 = ((bf16[32,64,512]{2,1,0:T(8,128)(2,1)}), bf16[32,64,512]{2,1,0:T(8,128)(2,1)}, u32[]{:S(2)}, u32[]{:S(2)}) async-start(bf16[32,64,512]{2,1,0:T(8,128)(2,1)} %bitcast.313), calls=%async_computation.9 | async-start | bytes 4194304 | tf_op jit(solution)/shard_map/all_to_all | solution.py:30
  217.3 28.8 %all-to-all-start.6 = ((bf16[32,120,128]{2,1,0:T(8,128)(2,1)}), bf16[32,120,128]{2,1,0:T(8,128)(2,1)S(1)}, u32[]{:S(2)}, u32[]{:S(2)}) async-start(bf16[32,120,128]{2,1,0:T(8,128)(2,1)} %bitcast.333), calls=%async_computation.6 | async-start | bytes 1966080 | tf_op jit(solution)/shard_map/all_to_all | solution.py:30
  219.9 55.8 %copy-start.64 = (f32[32]{0:T(128)}, f32[32]{0:T(128)S(1)}, u32[]{:S(2)}) copy-start(f32[32]{0:T(128)S(1)} %compare_convert_fusion) | copy-start | bytes 388
  225.9 20.2 %copy-start.63 = (bf16[128,32]{0,1:T(8,128)(2,1)S(1)}, bf16[128,32]{0,1:T(8,128)(2,1)}, u32[]{:S(2)}) copy-start(bf16[128,32]{0,1:T(8,128)(2,1)} %param.20) | copy-start | bytes 24580
  246.7 27.3 %all-to-all-start.7 = ((bf16[4,32,128]{2,1,0:T(8,128)(2,1)}), bf16[4,32,128]{2,1,0:T(8,128)(2,1)S(1)}, u32[]{:S(2)}, u32[]{:S(2)}) async-start(bf16[4,32,128]{2,1,0:T(8,128)(2,1)} %broadcast_in_dim.34), calls=%async_computation.7 | async-start | bytes 65536 | tf_op jit(solution)/shard_map/all_to_all | solution.py:58
  275.7 17.9 %copy-start.28 = (f32[960,32]{0,1:T(8,128)}, f32[960,32]{0,1:T(8,128)S(1)}, u32[]{:S(2)}) copy-start(f32[960,32]{0,1:T(8,128)S(1)} %get-tuple-element.112) | copy-start | bytes 368644
  278.1 8.1 %copy-start.19 = (bf16[64,8,8,256]{3,1,2,0:T(8,128)(2,1)S(1)}, bf16[64,8,8,256]{3,1,2,0:T(8,128)(2,1)}, u32[]{:S(2)}) copy-start(bf16[64,8,8,256]{3,1,2,0:T(8,128)(2,1)} %copy.280) | copy-start | bytes 6291460
  293.6 5.1 copy-start.34
  295.5 29.5 %all-to-all-start.13 = ((bf16[32,120,128]{2,1,0:T(8,128)(2,1)}), bf16[32,120,128]{2,1,0:T(8,128)(2,1)S(1)}, u32[]{:S(2)}, u32[]{:S(2)}) async-start(bf16[32,120,128]{2,1,0:T(8,128)(2,1)} %bitcast.45), calls=%async_computation.13 | async-start | bytes 1966080 | tf_op jit(solution)/shard_map/all_to_all | solution.py:30
  324.9 10.4 %all-to-all-start.11 = ((bf16[4,394,128]{2,1,0:T(8,128)(2,1)}), bf16[4,394,128]{2,1,0:T(8,128)(2,1)S(1)}, u32[]{:S(2)}, u32[]{:S(2)}) async-start(bf16[4,394,128]{2,1,0:T(8,128)(2,1)} %reshape.316), calls=%async_computation.11 | async-start | bytes 819200 | tf_op jit(solution)/shard_map/all_to_all | solution.py:77
  334.4 5.6 copy-start.26
  335.3 10.5 %all-to-all-start.14 = ((bf16[4,394,128]{2,1,0:T(8,128)(2,1)}), bf16[4,394,128]{2,1,0:T(8,128)(2,1)S(1)}, u32[]{:S(2)}, u32[]{:S(2)}) async-start(bf16[4,394,128]{2,1,0:T(8,128)(2,1)} %reshape.321), calls=%async_computation.14 | async-start | bytes 819200 | tf_op jit(solution)/shard_map/all_to_all | solution.py:77
  344.0 6.7 %copy-start.41 = (f32[1,4,128]{2,0,1:T(1,128)S(1)}, f32[1,4,128]{2,0,1:T(1,128)}, u32[]{:S(2)}) copy-start(f32[1,4,128]{2,0,1:T(1,128)} %copy-done.40) | copy-start | bytes 6148
  344.0 6.7 %copy-start.54 = (f32[394]{0:T(512)S(1)}, f32[394]{0:T(512)}, u32[]{:S(2)}) copy-start(f32[394]{0:T(512)} %copy-done.53) | copy-start | bytes 4732
  345.8 18.2 %all-to-all-start.4 = ((bf16[4,394,128]{2,1,0:T(8,128)(2,1)}), bf16[4,394,128]{2,1,0:T(8,128)(2,1)}, u32[]{:S(2)}, u32[]{:S(2)}) async-start(bf16[4,394,128]{2,1,0:T(8,128)(2,1)} %bitcast.286), calls=%async_computation.4 | async-start | bytes 819200 | tf_op jit(solution)/shard_map/all_to_all | solution.py:85
  353.3 6.7 %copy-start.1 = (f32[2,8,197,197]{2,3,1,0:T(8,128)S(1)}, f32[2,8,197,197]{2,3,1,0:T(8,128)}, u32[]{:S(2)}) copy-start(f32[2,8,197,197]{2,3,1,0:T(8,128)} %copy-done) | copy-start | bytes 7451332
  364.0 29.6 %all-to-all-start.10 = ((bf16[32,120,128]{2,1,0:T(8,128)(2,1)}), bf16[32,120,128]{2,1,0:T(8,128)(2,1)}, u32[]{:S(2)}, u32[]{:S(2)}) async-start(bf16[32,120,128]{2,1,0:T(8,128)(2,1)} %bitcast.36), calls=%async_computation.10 | async-start | bytes 1966080 | tf_op jit(solution)/shard_map/all_to_all | solution.py:30
  378.4 18.9 %copy-start.30 = (bf16[8,120,4,128]{3,2,1,0:T(4,128)(2,1)S(1)}, bf16[8,120,4,128]{3,2,1,0:T(4,128)(2,1)}, u32[]{:S(2)}) copy-start(bf16[8,120,4,128]{3,2,1,0:T(4,128)(2,1)} %copy-done.29) | copy-start | bytes 2949124
  393.5 10.7 %all-to-all-start.15 = ((bf16[4,394,128]{2,1,0:T(8,128)(2,1)}), bf16[4,394,128]{2,1,0:T(8,128)(2,1)S(1)}, u32[]{:S(2)}, u32[]{:S(2)}) async-start(bf16[4,394,128]{2,1,0:T(8,128)(2,1)} %bitcast.284), calls=%async_computation.15 | async-start | bytes 819200 | tf_op jit(solution)/shard_map/all_to_all | solution.py:85
  402.4 5.9 %copy-start.50 = (f32[960]{0:T(1024)S(1)}, f32[960]{0:T(1024)}, u32[]{:S(2)}) copy-start(f32[960]{0:T(1024)} %copy-done.48) | copy-start | bytes 11524
  405.1 53.4 %all-to-all-start.17 = ((bf16[32,128,256]{2,1,0:T(8,128)(2,1)}), bf16[32,128,256]{2,1,0:T(8,128)(2,1)S(1)}, u32[]{:S(2)}, u32[]{:S(2)}) async-start(bf16[32,128,256]{2,1,0:T(8,128)(2,1)} %bitcast.294), calls=%async_computation.17 | async-start | bytes 4194304 | tf_op jit(solution)/shard_map/all_to_all | solution.py:30
  419.4 42.8 %copy-start.23 = (bf16[50,8,4,128]{3,1,2,0:T(8,128)(2,1)S(1)}, bf16[50,8,4,128]{3,1,2,0:T(8,128)(2,1)}, u32[]{:S(2)}) copy-start(bf16[50,8,4,128]{3,1,2,0:T(8,128)(2,1)} %copy-done.22) | copy-start | bytes 1228804
  419.4 43.6 %copy-start.44 = (f32[960]{0:T(1024)S(1)}, f32[960]{0:T(1024)}, u32[]{:S(2)}) copy-start(f32[960]{0:T(1024)} %copy-done.42) | copy-start | bytes 11524
  419.4 43.6 %copy-start.47 = (f32[960]{0:T(1024)S(1)}, f32[960]{0:T(1024)}, u32[]{:S(2)}) copy-start(f32[960]{0:T(1024)} %copy-done.45) | copy-start | bytes 11524
  419.4 43.6 %copy-start.61 = (f32[960]{0:T(1024)S(1)}, f32[960]{0:T(1024)}, u32[]{:S(2)}) copy-start(f32[960]{0:T(1024)} %copy-done.60) | copy-start | bytes 11524
  419.4 43.6 %copy-start.66 = (f32[32]{0:T(128)S(1)}, f32[32]{0:T(128)}, u32[]{:S(2)}) copy-start(f32[32]{0:T(128)} %copy-done.64) | copy-start | bytes 388
  422.9 42.4 %copy-start.21 = (bf16[512,394]{0,1:T(8,128)(2,1)S(1)}, bf16[512,394]{0,1:T(8,128)(2,1)}, u32[]{:S(2)}) copy-start(bf16[512,394]{0,1:T(8,128)(2,1)} %get-tuple-element.85) | copy-start | bytes 1210372
  458.4 12.0 %copy-start.3 = (bf16[32,128,256]{2,1,0:T(8,128)(2,1)}, bf16[32,128,256]{2,1,0:T(8,128)(2,1)S(1)}, u32[]{:S(2)}) copy-start(bf16[32,128,256]{2,1,0:T(8,128)(2,1)S(1)} %all-to-all-done.17) | copy-start | bytes 6291460
  458.4 7.8 %copy-start.11 = (bf16[394,512]{0,1:T(8,128)(2,1)S(1)}, bf16[394,512]{0,1:T(8,128)(2,1)}, u32[]{:S(2)}) copy-start(bf16[394,512]{0,1:T(8,128)(2,1)} %copy-done.10) | copy-start | bytes 1210372
  458.4 53.8 %all-to-all-start.18 = ((bf16[32,64,512]{2,1,0:T(8,128)(2,1)}), bf16[32,64,512]{2,1,0:T(8,128)(2,1)}, u32[]{:S(2)}, u32[]{:S(2)}) async-start(bf16[32,64,512]{2,1,0:T(8,128)(2,1)} %bitcast.291), calls=%async_computation.18 | async-start | bytes 4194304 | tf_op jit(solution)/shard_map/all_to_all | solution.py:30
  472.8 44.7 %copy-start.36 = (bf16[1576,128]{1,0:T(8,128)(2,1)S(1)}, bf16[1576,128]{1,0:T(8,128)(2,1)}, u32[]{:S(2)}) copy-start(bf16[1576,128]{1,0:T(8,128)(2,1)} %param.13) | copy-start | bytes 1210372
  512.2 60.4 %all-to-all-start.16 = ((bf16[32,292,128]{2,1,0:T(8,128)(2,1)}), bf16[32,292,128]{2,1,0:T(8,128)(2,1)S(1)}, u32[]{:S(2)}, u32[]{:S(2)}) async-start(bf16[32,292,128]{2,1,0:T(8,128)(2,1)} %copy.253), calls=%async_computation.16 | async-start | bytes 4849664 | tf_op jit(solution)/shard_map/all_to_all | solution.py:267
  517.4 7.3 %copy-start.25 = (bf16[4,394,128]{2,1,0:T(8,128)(2,1)S(1)}, bf16[4,394,128]{2,1,0:T(8,128)(2,1)}, u32[]{:S(2)}) copy-start(bf16[4,394,128]{2,1,0:T(8,128)(2,1)} %copy-done.24) | copy-start | bytes 1210372
  (39 other events, 96.7 us)

commit v2 on v1

--- a/solution.py
+++ b/solution.py
@@ -53,36 +53,109 @@
     return lax.psum_scatter(x, "col", scatter_dimension=0, axis_index_groups=far_groups())
 
 
-def spread(x, axis, groups=None):
-    n = len(groups[0]) if groups else lax.axis_size(axis)
-    return lax.all_to_all(
-        jnp.broadcast_to(x[None], (n,) + x.shape), axis, 0, 0, tiled=True, axis_index_groups=groups
-    )
+def after(x, *earlier):
+    return lax.optimization_barrier((x,) + earlier)[0]
+
+
+def swaps(axis, distance):
+    return [(i, i ^ distance) for i in range(lax.axis_size(axis))]
+
+
+def pick(pieces, at):
+    return lax.dynamic_index_in_dim(pieces, at, 0, keepdims=False)
+
+
+def in_order(got, here):
+    pieces, step = list(got), 1
+    while step < len(pieces):
+        odd = (here & step) != 0
+        pieces = [jnp.where(odd, pieces[k ^ step], pieces[k]) for k in range(len(pieces))]
+        step *= 2
+    return pieces
+
+
+def row_exchange(pieces):
+    here = lax.axis_index("row")
+    got = [pick(pieces, here)]
+    for k in range(1, lax.axis_size("row")):
+        got.append(lax.ppermute(pick(pieces, here ^ k), "row", swaps("row", k)))
+    return in_order(got, here)
+
+
+def row_spread(x):
+    got = [x] + [lax.ppermute(x, "row", swaps("row", k)) for k in range(1, lax.axis_size("row"))]
+    return jnp.stack(in_order(got, lax.axis_index("row")))
+
+
+def parity_groups():
+    cols = lax.axis_size("col")
+    return [[2 * i + k for i in range(cols // 2)] for k in range(2)]
+
+
+def far_spread(x):
+    half = lax.axis_size("col") // 2
+    if half > 8:
+        return lax.all_gather(x, "col", axis=0, axis_index_groups=parity_groups())
+    got = [x] + [lax.ppermute(x, "col", swaps("col", 2 * k)) for k in range(1, half)]
+    return jnp.stack(in_order(got, lax.axis_index("col") // 2))
+
+
+def far_sum(pieces):
+    half = lax.axis_size("col") // 2
+    if half > 8:
+        got = lax.all_to_all(pieces, "col", 0, 0, tiled=True, axis_index_groups=parity_groups())
+        return jnp.sum(got.astype(F32), axis=0)
+    here = lax.axis_index("col") // 2
+    total = pick(pieces, here).astype(F32)
+    for k in range(1, half):
+        sent = lax.ppermute(pick(pieces, here ^ k), "col", swaps("col", 2 * k))
+        total = total + sent.astype(F32)
+    return total
 
 
 def gather_all(x):
     half = lax.axis_size("col") // 2
-    far = spread(x, "col", [[2 * i + k for i in range(half)] for k in range(2)])
-    mine = spread(far, "row")
-    swap = [(i, i ^ 1) for i in range(2 * half)]
-    other = lax.ppermute(mine, "col", swap)
+    mine = row_spread(far_spread(x))
+    other = lax.ppermute(mine, "col", swaps("col", 1))
     first = lax.axis_index("col") % 2 == 0
     both = jnp.stack([jnp.where(first, mine, other), jnp.where(first, other, mine)], axis=2)
     return both.reshape((both.shape[0], 2 * half) + x.shape)
 
 
+def reduce_all(x):
+    cols, n, width = x.shape
+    rows = lax.axis_size("row")
+    core = lax.axis_index("col") % 2
+    pairs = x.reshape(cols // 2, 2, n, width).transpose(1, 0, 2, 3).astype(BF16)
+    sent = lax.ppermute(pick(pairs, 1 - core), "col", swaps("col", 1))
+    mine = pick(pairs, core).astype(F32) + sent.astype(F32)
+    mine = mine.astype(BF16).reshape(cols // 2, n, rows, width // rows).transpose(2, 0, 1, 3)
+    mine = sum(piece.astype(F32) for piece in row_exchange(mine))
+    return far_sum(mine.astype(BF16))
+
+
+def pack_in(x, chunks):
+    e, n, h = x.shape
+    return x.reshape(e, chunks, n // chunks, h).transpose(0, 2, 1, 3).reshape(e, n // chunks, -1)
+
+
+def unpack_in(x, chunks):
+    e, n, h = x.shape
+    x = x.reshape(e, n, chunks, h // chunks).transpose(0, 2, 1, 3)
+    return x.reshape(e, n * chunks, h // chunks)
+
+
 def to_tokens(x):
     rows = lax.axis_size("row")
     t, w = x.shape
-    y = lax.all_to_all(x.reshape(rows, t // rows, w), "row", 0, 0, tiled=True)
-    return y.transpose(1, 0, 2).reshape(t // rows, rows * w)
+    return jnp.concatenate(row_exchange(x.reshape(rows, t // rows, w)), axis=1)
 
 
 def to_features(x):
     rows = lax.axis_size("row")
     t, w = x.shape
     y = x.reshape(t, rows, w // rows).transpose(1, 0, 2)
-    return lax.all_to_all(y, "row", 0, 0, tiled=True).reshape(t * rows, w // rows)
+    return jnp.concatenate(row_exchange(y), axis=0)
 
 
 def normalize(values):
@@ -153,26 +226,32 @@
     small = gather_all(jnp.concatenate([qkv_weight.T, out_weight.T], axis=0))
     qkv_t = small[:, :, :qkv_part].transpose(1, 2, 0, 3).reshape(3 * width, width)
     mix_t = small[:, :, qkv_part:].transpose(1, 2, 0, 3).reshape(width, width)
-    norms = spread(jnp.stack([ln1_gain, ln1_bias, ln2_gain, ln2_bias]), "row")
+    norms = row_spread(jnp.stack([ln1_gain, ln1_bias, ln2_gain, ln2_bias]))
     norms = norms.transpose(1, 0, 2).reshape(4, width)
-    router_t = spread(router_weight.T, "row").transpose(1, 0, 2).reshape(E, width)
-    w_in = exchange(expert_in).reshape(rows, near, width_part, hid_part)
+    router_t = row_spread(router_weight.T).transpose(1, 0, 2).reshape(E, width)
+    chunks = width_part // out_part
+    w_sent = jnp.concatenate([pack_in(expert_in, chunks), expert_out.transpose(0, 2, 1)], axis=1)
+    w_got = exchange(w_sent)
+    w_in = unpack_in(w_got[:, :out_part], chunks).reshape(rows, near, width_part, hid_part)
     w_in = collect_far(w_in).transpose(1, 3, 0, 2, 4).reshape(width, hid)
-    w_out_t = exchange(expert_out.transpose(0, 2, 1)).reshape(rows, near, out_part, hid // rows)
+    w_out_t = w_got[:, out_part:].reshape(rows, near, out_part, hid // rows)
     w_out_t = collect_far(w_out_t).transpose(0, 2, 3, 1, 4).reshape(width, hid)
 
-    def dispatch(values):
-        picked = dot(hits, values, ((0,), (0,))).astype(BF16)
-        got = exchange(picked.reshape(E, CAP, width_part))
+    def to_slots(values):
+        return dot(hits, values, ((0,), (0,))).astype(BF16).reshape(E, CAP, width_part)
+
+    def to_rows(got):
         got = got.reshape(rows, near, CAP, width_part).transpose(1, 2, 0, 3)
         return got.reshape(near * CAP, width)
 
-    def combine(values):
+    def from_rows(values):
         sent = values.astype(BF16).reshape(near, CAP, rows, width_part).transpose(2, 0, 1, 3)
-        got = exchange(sent.reshape(E, CAP, width_part))
+        return sent.reshape(E, CAP, width_part)
+
+    def from_slots(got):
         return dot(hits, got.reshape(E * CAP, width_part), ((1,), (0,)))
 
-    cot_rows = dispatch(cotangent).astype(F32)
+    cot_sent = to_slots(cotangent)
     tok_float = to_tokens(tokens).astype(F32)
     grad_out = to_tokens(cotangent).astype(F32)
 
@@ -194,7 +273,10 @@
     normed2 = (normal2 * norms[2] + norms[3]).astype(BF16)
     attn_part = to_features(attn_out.astype(BF16))
 
-    x_rows = dispatch(to_features(normed2))
+    x_got = exchange(after(to_slots(to_features(normed2)), w_got))
+    x_rows = to_rows(x_got)
+    cot_got = exchange(after(cot_sent, x_got))
+    cot_rows = to_rows(cot_got).astype(F32)
     flat = lax.axis_index("row") * near + lax.axis_index("col") % near
     gates = softmax_last(dot(x_rows, router_t, ((1,), (1,))))
     own = (jnp.arange(E) == flat).astype(F32)[None, :]
@@ -210,18 +292,21 @@
     (grad_pre,) = gelu_back(grad_act)
     grad_pre = grad_pre.astype(BF16)
     grad_rows = dot(grad_pre, w_in, ((1,), (1,))) + dot(grad_logits, router_t, ((1,), (0,)))
-    grad_norm2 = to_tokens(combine(grad_rows).astype(BF16)).astype(F32)
-    moved = combine(chosen * expert_res)
-    layer_out = (tokens.astype(F32) + attn_part.astype(F32) + moved).astype(BF16)
+    moved_got = exchange(after(from_rows(chosen * expert_res), cot_got))
+    grad_got = exchange(after(from_rows(grad_rows), moved_got))
+    grad_norm2 = to_tokens(from_slots(grad_got).astype(BF16)).astype(F32)
+    layer_out = (tokens.astype(F32) + attn_part.astype(F32) + from_slots(moved_got)).astype(BF16)
     router_part = dot(grad_logits, x_rows, ((0,), (0,)))
     out_grad_t = dot(grad_res, activated, ((0,), (0,))).astype(BF16)
     in_grad = dot(x_rows, grad_pre, ((0,), (0,))).astype(BF16)
-    out_grad_t = out_grad_t.reshape(groups, near, out_part, rows, hid // rows).transpose(0, 3, 1, 2, 4)
-    out_grad_t = exchange(reduce_far(out_grad_t).reshape(E, out_part, hid // rows))
+    out_grad_t = out_grad_t.reshape(groups, near, out_part, rows, hid // rows)
+    out_grad_t = reduce_far(out_grad_t.transpose(0, 3, 1, 2, 4)).reshape(E, out_part, hid // rows)
     in_grad = in_grad.reshape(rows, width_part, groups, near, hid_part).transpose(2, 0, 3, 1, 4)
-    in_grad = exchange(reduce_far(in_grad).reshape(E, width_part, hid_part))
-    expert_out_grad = out_grad_t.astype(F32).transpose(0, 2, 1)
-    expert_in_grad = in_grad.astype(F32)
+    in_grad = reduce_far(in_grad).reshape(E, width_part, hid_part)
+    w_grads = jnp.concatenate([pack_in(in_grad, chunks), out_grad_t], axis=1)
+    w_grads = exchange(after(w_grads, grad_got)).astype(F32)
+    expert_out_grad = w_grads[:, out_part:].transpose(0, 2, 1)
+    expert_in_grad = unpack_in(w_grads[:, :out_part], chunks)
 
     gain2_part = jnp.sum(grad_norm2 * normal2, axis=0)
     bias2_part = jnp.sum(grad_norm2, axis=0)
@@ -260,12 +345,8 @@
             ),
         ],
         axis=1,
-    ).astype(BF16)
-    depth = shares.shape[1]
-    shares = shares.reshape(cols, depth, rows, width_part).transpose(2, 0, 1, 3)
-    shares = shares.reshape(rows * cols, depth, width_part)
-    shares = lax.all_to_all(shares, ("row", "col"), 0, 0, tiled=True)
-    sums = jnp.sum(shares.astype(F32), axis=0)
+    )
+    sums = reduce_all(shares)
     thin = width_part // cols
     tail = lax.dynamic_slice_in_dim(
         sums[qkv_part + mix_part :], lax.axis_index("col") * thin, thin, axis=1

time: 584 us -> 478 us (0.82)
  waiting for transfers between devices: 218 us -> 127 us
  blocking collectives: 65.7 us -> 0 us
  local copies, waits for them, and re-layouts: 81.1 us -> 106 us
  starting transfers between devices: 65.8 us -> 90.1 us
  other arithmetic: 40.1 us -> 51.4 us
  matrix products: 104 us -> 96.3 us
    all_to_all x7 -> x6, waiting for transfers between devices: 169 us -> 17.1 us  [exchange(): return lax.all_to_all(pieces, ('row', 'col'), 0, 0, tiled=True)]
    ppermute x1 -> x38, waiting for transfers between devices: 0.01 us -> 110 us  [the longest x3 62.8 us: far_spread(): lax.ppermute(x, 'col', swaps('col', 2 * k))]
    all_to_all x2 -> x0, blocking collectives: 65.7 us -> none  [the longest x1 53.9 us: exchange(): return lax.all_to_all(pieces, ('row', 'col'), 0, 0, tiled=True)]
    ppermute x1 -> x38, starting transfers between devices: 0.07 us -> 56.4 us  [the longest x21 28.2 us: row_exchange(): got.append(lax.ppermute(pick(pieces, here ^ k), 'row', swaps('row', k)))]
    all_to_all x10 -> x0, waiting for transfers between devices: 49.3 us -> none  [the longest x1 38.6 us: local(): shares = lax.all_to_all(shares, ('row', 'col'), 0, 0, tiled=True)]
    all_to_all x10 -> x0, starting transfers between devices: 40.8 us -> none  [the longest x4 17.2 us: spread(): lax.all_to_all(jnp.broadcast_to(x[None], (n,) + x.shape), axis, 0, 0, til...]
    reshape x10 -> x15, local copies, waits for them, and re-layouts: 13.9 us -> 30.2 us  [the longest x2 8.65 us: unpack_in(): x = x.reshape(e, n, chunks, h // chunks).transpose(0, 2, 1, 3)]
    concatenate x0 -> x3, other arithmetic: none -> 9.13 us  [the longest x1 4.67 us: local(): jnp.concatenate([pack_in(expert_in, chunks), expert_out.transpose(0, 2, 1...]
  transfers between devices with their start and end apart: 18 -> 44, of which waited for: 10 -> 13; matrix products, arithmetic and copies ran while one was open for 33% -> 43% of each run, Pallas kernels for 0% -> 0%
where the time goes in v2:
time: 478 us; the launch traced here: 474 us
  waiting for transfers between devices  127 us (27%)
  local copies, waits for them, and re-layouts  106 us (22%)
  matrix products  96.3 us (20%)
  starting transfers between devices  90.1 us (19%)
  other arithmetic  51.4 us (11%)
    dot_general x20, matrix products, dot(): return lax.dot_general(a, b, (dims, ((), ())), preferred_element_type=F32)  90.6 us
    ppermute x3, waiting for transfers between devices, far_spread(): lax.ppermute(x, 'col', swaps('col', 2 * k))  62.8 us
    all_to_all x6, starting transfers between devices, exchange(): return lax.all_to_all(pieces, ('row', 'col'), 0, 0, tiled=True)  33.7 us
    ppermute x21, starting transfers between devices, row_exchange(): got.append(lax.ppermute(pick(pieces, here ^ k), 'row', swaps('row', k)))  28.2 us
    ppermute x21, waiting for transfers between devices, row_exchange(): got.append(lax.ppermute(pick(pieces, here ^ k), 'row', swaps('row', k)))  22.8 us
    unnamed x175, local copies, waits for them, and re-layouts  18.2 us
    all_to_all x6, waiting for transfers between devices, exchange(): return lax.all_to_all(pieces, ('row', 'col'), 0, 0, tiled=True)  17.1 us
    reduce_or x1, other arithmetic, local(): jnp.any(slots[:, :, None] == jnp.arange(E * CAP, dtype=jnp.int32)[None, N...  17.1 us
  transfers between devices with their start and end apart: 44, of which 13 were waited for; matrix products, arithmetic and copies ran while one was open for 43% of the time, Pallas kernels for 0%

profile of v2, /device:TPU:0, one launch (start us, length us, event | category | flops | bytes accessed | tf_op | source)
XLA Modules:
  0.0 473.7 jit_solution(16324337970592220242)
XLA Ops:
  1.5 5.0 %collective-permute-start.6 = (bf16[256,128]{1,0:T(8,128)(2,1)S(1)}, bf16[256,128]{1,0:T(8,128)(2,1)S(1)}, u32[]{:S(2)}, u32[]{:S(2)}) collective-permute-start(bf16[256,128]{1,0:T(8,128)(2,1)S(1)} %pad_maximum_fusion.8), channel_id=1, source_target_pairs={{0,6},{1,7},{2,4},{3,5},{4,2},{5,3},{6,0},{7,1},{8,14},{9,15},{10,... | collective-permute-start | bytes 196616 | tf_op jit(solution)/shard_map/ppermute | solution.py:99
  10.8 3.8 copy.421
  14.6 2.6 reshape.273
  17.2 4.7 pad_maximum_fusion
  21.9 5.5 %all-to-all-start = ((bf16[32,128,512]{2,1,0:T(8,128)(2,1)}), bf16[32,128,512]{2,1,0:T(8,128)(2,1)}, u32[]{:S(2)}, u32[]{:S(2)}) async-start(bf16[32,128,512]{2,1,0:T(8,128)(2,1)} %pad_maximum_fusion), calls=%async_computation | async-start | bytes 8388608 | tf_op jit(solution)/shard_map/all_to_all | solution.py:30
  34.4 62.8 %collective-permute-done.8 = bf16[256,128]{1,0:T(8,128)(2,1)S(1)} collective-permute-done((bf16[256,128]{1,0:T(8,128)(2,1)S(1)}, bf16[256,128]{1,0:T(8,128)(2,1)S(1)}, u32[]{:S(2)}, u32[]{:S(2)}) %collective-permute-start.8) | collective-permute-done | bytes 65568 | tf_op jit(solution)/shard_map/ppermute | solution.py:99
  100.9 7.2 %collective-permute-done.10 = bf16[4,256,128]{2,1,0:T(8,128)(2,1)S(1)} collective-permute-done((bf16[4,256,128]{2,1,0:T(8,128)(2,1)S(1)}, bf16[4,256,128]{2,1,0:T(8,128)(2,1)S(1)}, u32[]{:S(2)}, u32[]{:S(2)}) %collective-permute-start.10) | collective-permute-done | bytes 262176 | tf_op jit(solution)/shard_map/ppermute | solution.py:86
  108.1 3.9 collective-permute-start.2
  114.1 3.0 collective-permute-done.9
  125.0 3.1 reshape.305
  134.3 3.0 fusion.100
  148.2 17.1 %fusion.1 = pred[1576,3840]{1,0:T(8,128)(4,1)} fusion(s32[1576,2]{0,1:T(2,128)S(1)} %copy-done.50), kind=kLoop, calls=%fused_computation.2 | loop fusion | flops 18155520 | bytes 6064448 | tf_op jit(solution)/shard_map/reduce_or | solution.py:222
  168.2 10.6 %convolution_convert_fusion.1 = bf16[3840,128]{1,0:T(8,128)(2,1)} fusion(pred[1576,3840]{1,0:T(8,128)(4,1)} %fusion.1, bf16[1576,128]{1,0:T(8,128)(2,1)S(1)} %concatenate.34), kind=kOutput, calls=%fused_computation.23 | convolution fusion | flops 1549762560 | bytes 7438336 | tf_op jit(solution)/shard_map/dot_general | solution.py:18
  178.9 8.0 %all-to-all-start.1 = ((bf16[32,120,128]{2,1,0:T(8,128)(2,1)}), bf16[32,120,128]{2,1,0:T(8,128)(2,1)}, u32[]{:S(2)}, u32[]{:S(2)}) async-start(bf16[32,120,128]{2,1,0:T(8,128)(2,1)} %bitcast.45), calls=%async_computation.1 | async-start | bytes 1966080 | tf_op jit(solution)/shard_map/all_to_all | solution.py:30
  186.8 10.5 %convolution_convert_fusion = bf16[3840,128]{1,0:T(8,128)(2,1)} fusion(pred[1576,3840]{1,0:T(8,128)(4,1)} %fusion.1, bf16[1576,128]{1,0:T(8,128)(2,1)S(1)} %copy-done.44), kind=kOutput, calls=%fused_computation.22 | convolution fusion | flops 1549762560 | bytes 7438336 | tf_op jit(solution)/shard_map/dot_general | solution.py:18
  199.0 4.7 fusion.97
  203.8 2.7 reshape.277
  215.7 6.2 %all-to-all-start.2 = ((bf16[32,120,128]{2,1,0:T(8,128)(2,1)}), bf16[32,120,128]{2,1,0:T(8,128)(2,1)S(1)}, u32[]{:S(2)}, u32[]{:S(2)}) async-start(bf16[32,120,128]{2,1,0:T(8,128)(2,1)} %bitcast.460), calls=%async_computation.2 | async-start | bytes 1966080 | tf_op jit(solution)/shard_map/all_to_all | solution.py:30
  221.9 21.9 %multiply_convert_fusion = (bf16[960,2048]{1,0:T(8,128)(2,1)}, f32[960,2048]{1,0:T(8,128)}, f32[960,2048]{1,0:T(8,128)}) fusion(bf16[512,2048]{1,0:T(8,128)(2,1)} %bitcast.443, bf16[120,8,4,128]{3,2,1,0:T(4,128)(2,1)S(1)} %bitcast.456), kind=kOutput, calls=%fused_computation.8 | convolution fusion | flops 2141061120 | bytes 22740992 | tf_op jit(solution)/shard_map/dot_general | solution.py:18
  244.5 3.6 all-to-all-done.2
  251.5 3.2 fusion.15
  257.8 3.8 all-to-all-start.3
  261.7 8.5 %add_convert_fusion = bf16[960,2048]{1,0:T(8,128)(2,1)S(1)} fusion(f32[960,2048]{1,0:T(8,128)} %get-tuple-element.86, f32[960,2048]{1,0:T(8,128)} %get-tuple-element.179, bf16[512,2048]{1,0:T(8,128)(2,1)} %bitcast.445, bf16[120,8,4,128]{3,2,1,0:T(4,128)(2,1)S(1)} %bitcast.461), kind=kOutput, calls=%fused_computation.7 | convolution fusion | flops 2040791040 | bytes 22740992 | tf_op jit(solution)/shard_map/dot_general | solution.py:18
  274.3 13.5 %all-to-all-done.3 = bf16[32,120,128]{2,1,0:T(8,128)(2,1)} async-done(((bf16[32,120,128]{2,1,0:T(8,128)(2,1)}), bf16[32,120,128]{2,1,0:T(8,128)(2,1)}, u32[]{:S(2)}, u32[]{:S(2)}) %all-to-all-start.3) | async-done | bytes 983072 | tf_op jit(solution)/shard_map/all_to_all | solution.py:30
  287.8 3.4 all-to-all-start.4
  294.8 9.7 %collective-permute-done.22 = bf16[394,128]{1,0:T(8,128)(2,1)S(1)} collective-permute-done((bf16[394,128]{1,0:T(8,128)(2,1)S(1)}, bf16[394,128]{1,0:T(8,128)(2,1)S(1)}, u32[]{:S(2)}, u32[]{:S(2)}) %collective-permute-start.22) | collective-permute-done | bytes 100896 | tf_op jit(solution)/shard_map/ppermute | solution.py:81
  306.6 4.8 %convolution_convert_fusion.3 = bf16[512,2048]{1,0:T(8,128)(2,1)S(1)} fusion(bf16[960,2048]{1,0:T(8,128)(2,1)} %copy-done.75, bf16[120,8,4,128]{3,2,1,0:T(4,128)(2,1)} %bitcast.458), kind=kOutput, calls=%fused_computation.32 | convolution fusion | flops 2014314496 | bytes 7012352 | tf_op jit(solution)/shard_map/dot_general | solution.py:18
  315.6 3.9 convolution_convert_fusion.2
  319.5 3.3 reshape.294
  325.6 7.2 %convolution_convert_fusion.5 = bf16[1576,128]{1,0:T(8,128)(2,1)} fusion(pred[1576,3840]{1,0:T(8,128)(4,1)} %fusion.1, bf16[3840,128]{1,0:T(8,128)(2,1)} %bitcast.76), kind=kOutput, calls=%fused_computation.39 | convolution fusion | flops 1549472768 | bytes 7438336 | tf_op jit(solution)/shard_map/dot_general | solution.py:18
  339.9 4.0 pad_maximum_fusion.1
  343.9 6.9 %all-to-all-start.5 = ((bf16[32,128,512]{2,1,0:T(8,128)(2,1)}), bf16[32,128,512]{2,1,0:T(8,128)(2,1)}, u32[]{:S(2)}, u32[]{:S(2)}) async-start(bf16[32,128,512]{2,1,0:T(8,128)(2,1)} %pad_maximum_fusion.1), calls=%async_computation.5 | async-start | bytes 8388608 | tf_op jit(solution)/shard_map/all_to_all | solution.py:30
  355.0 2.8 multiply_reduce_fusion
  366.3 3.9 fusion.53
  376.9 2.6 collective-permute-start.13
  384.2 2.7 collective-permute-start.28
  387.5 3.1 fusion.12
  390.6 2.6 reshape.304
  398.4 2.6 collective-permute-start.32
  401.9 5.7 %fusion.102 = f32[1576,128]{1,0:T(8,128)S(1)} fusion(pred[1576,3840]{1,0:T(8,128)(4,1)} %fusion.1, bf16[3840,128]{1,0:T(8,128)(2,1)} %bitcast.65), kind=kOutput, calls=%fused_computation.318 | convolution fusion | flops 1549271040 | bytes 7841792 | tf_op jit(solution)/shard_map/dot_general | solution.py:18
  410.4 6.6 %collective-permute-done.32 = bf16[4,292,128]{2,1,0:T(8,128)(2,1)} collective-permute-done((bf16[4,292,128]{2,1,0:T(8,128)(2,1)}, bf16[4,292,128]{2,1,0:T(8,128)(2,1)}, u32[]{:S(2)}, u32[]{:S(2)}) %collective-permute-start.32) | collective-permute-done | bytes 299040 | tf_op jit(solution)/shard_map/ppermute | solution.py:81
  417.0 2.7 collective-permute-done.33
  423.5 6.9 %collective-permute-start.35 = (bf16[292,128]{1,0:T(8,128)(2,1)S(1)}, bf16[292,128]{1,0:T(8,128)(2,1)S(1)}, u32[]{:S(2)}, u32[]{:S(2)}) collective-permute-start(bf16[292,128]{1,0:T(8,128)(2,1)S(1)} %get-tuple-element.154), channel_id=1, source_target_pairs={{0,2},{1,3},{2,0},{3,1},{4,6},{5,7},{6,4},{7,5},{8,10},{9,11},{10,... | collective-permute-start | bytes 224264 | tf_op jit(solution)/shard_map/ppermute | solution.py:111
  436.4 13.6 %collective-permute-done.36 = bf16[292,128]{1,0:T(8,128)(2,1)S(1)} collective-permute-done((bf16[292,128]{1,0:T(8,128)(2,1)S(1)}, bf16[292,128]{1,0:T(8,128)(2,1)S(1)}, u32[]{:S(2)}, u32[]{:S(2)}) %collective-permute-start.36) | collective-permute-done | bytes 74784 | tf_op jit(solution)/shard_map/ppermute | solution.py:111
  452.7 4.2 slice.104
  456.8 5.9 %reshape.295 = f32[32,64,2,256]{3,2,1,0:T(2,128)} reshape(f32[32,64,512]{2,1,0:T(8,128)} %slice.104) | data formatting | bytes 8388608 | tf_op jit(solution)/shard_map/reshape | solution.py:144
  462.8 4.8 %copy.246 = f32[32,2,64,256]{3,2,1,0:T(8,128)} copy(f32[32,2,64,256]{3,1,2,0:T(2,128)} %bitcast.423) | data formatting | bytes 8388608 | tf_op jit(solution)/shard_map/transpose | solution.py:144
  467.6 3.3 convert_element_type.250
  (361 shorter events, 134.8 us)
Async XLA Ops:
  1.5 32.9 %collective-permute-start.6 = (bf16[256,128]{1,0:T(8,128)(2,1)S(1)}, bf16[256,128]{1,0:T(8,128)(2,1)S(1)}, u32[]{:S(2)}, u32[]{:S(2)}) collective-permute-start(bf16[256,128]{1,0:T(8,128)(2,1)S(1)} %pad_maximum_fusion.8), channel_id=1, source_target_pairs={{0,6},{1,7},{2,4},{3,5},{4,2},{5,3},{6,0},{7,1},{8,14},{9,15},{10,... | collective-permute-start | bytes 196616 | tf_op jit(solution)/shard_map/ppermute | solution.py:99
  6.5 27.9 %collective-permute-start.7 = (bf16[256,128]{1,0:T(8,128)(2,1)S(1)}, bf16[256,128]{1,0:T(8,128)(2,1)S(1)}, u32[]{:S(2)}, u32[]{:S(2)}) collective-permute-start(bf16[256,128]{1,0:T(8,128)(2,1)S(1)} %pad_maximum_fusion.8), channel_id=1, source_target_pairs={{0,4},{1,5},{2,6},{3,7},{4,0},{5,1},{6,2},{7,3},{8,12},{9,13},{10,... | collective-permute-start | bytes 196616 | tf_op jit(solution)/shard_map/ppermute | solution.py:99
  7.2 22.2 %collective-permute-start.3 = (f32[4,128]{1,0:T(4,128)S(1)}, f32[4,128]{1,0:T(4,128)S(1)}, u32[]{:S(2)}, u32[]{:S(2)}) collective-permute-start(f32[4,128]{1,0:T(4,128)S(1)} %pad_maximum_fusion.9), channel_id=1, source_target_pairs={{0,24},{8,16},{16,8},{24,0},{1,25},{9,17},{17,9},{25,1},{2,26},{10... | collective-permute-start | bytes 6152 | tf_op jit(solution)/shard_map/ppermute | solution.py:86
  9.7 21.7 %collective-permute-start.4 = (f32[4,128]{1,0:T(4,128)S(1)}, f32[4,128]{1,0:T(4,128)S(1)}, u32[]{:S(2)}, u32[]{:S(2)}) collective-permute-start(f32[4,128]{1,0:T(4,128)S(1)} %pad_maximum_fusion.9), channel_id=1, source_target_pairs={{0,16},{8,24},{16,0},{24,8},{1,17},{9,25},{17,1},{25,9},{2,18},{10... | collective-permute-start | bytes 6152 | tf_op jit(solution)/shard_map/ppermute | solution.py:86
  10.2 23.6 %collective-permute-start.5 = (f32[4,128]{1,0:T(4,128)S(1)}, f32[4,128]{1,0:T(4,128)S(1)}, u32[]{:S(2)}, u32[]{:S(2)}) collective-permute-start(f32[4,128]{1,0:T(4,128)S(1)} %pad_maximum_fusion.9), channel_id=1, source_target_pairs={{0,8},{8,0},{16,24},{24,16},{1,9},{9,1},{17,25},{25,17},{2,10},{10... | collective-permute-start | bytes 6152 | tf_op jit(solution)/shard_map/ppermute | solution.py:86
  21.9 157.0 %all-to-all-start = ((bf16[32,128,512]{2,1,0:T(8,128)(2,1)}), bf16[32,128,512]{2,1,0:T(8,128)(2,1)}, u32[]{:S(2)}, u32[]{:S(2)}) async-start(bf16[32,128,512]{2,1,0:T(8,128)(2,1)} %pad_maximum_fusion), calls=%async_computation | async-start | bytes 8388608 | tf_op jit(solution)/shard_map/all_to_all | solution.py:30
  27.4 69.8 %copy-start.45 = (bf16[128,192]{0,1:T(8,128)(2,1)S(1)}, bf16[128,192]{0,1:T(8,128)(2,1)}, u32[]{:S(2)}) copy-start(bf16[128,192]{0,1:T(8,128)(2,1)} %param.16) | copy-start | bytes 147460
  27.4 69.8 %copy-start.49 = (bf16[128,64]{0,1:T(8,128)(2,1)S(1)}, bf16[128,64]{0,1:T(8,128)(2,1)}, u32[]{:S(2)}) copy-start(bf16[128,64]{0,1:T(8,128)(2,1)} %param.17) | copy-start | bytes 49156
  29.5 67.7 %collective-permute-start.8 = (bf16[256,128]{1,0:T(8,128)(2,1)S(1)}, bf16[256,128]{1,0:T(8,128)(2,1)S(1)}, u32[]{:S(2)}, u32[]{:S(2)}) collective-permute-start(bf16[256,128]{1,0:T(8,128)(2,1)S(1)} %pad_maximum_fusion.8), channel_id=1, source_target_pairs={{0,2},{1,3},{2,0},{3,1},{4,6},{5,7},{6,4},{7,5},{8,10},{9,11},{10,... | collective-permute-start | bytes 196616 | tf_op jit(solution)/shard_map/ppermute | solution.py:99
  31.4 86.1 %collective-permute-start = (bf16[394,128]{1,0:T(8,128)(2,1)S(1)}, bf16[394,128]{1,0:T(8,128)(2,1)S(1)}, u32[]{:S(2)}, u32[]{:S(2)}) collective-permute-start(bf16[394,128]{1,0:T(8,128)(2,1)S(1)} %get-tuple-element.141), channel_id=1, source_target_pairs={{0,24},{8,16},{16,8},{24,0},{1,25},{9,17},{17,9},{25,1},{2,26},{10... | collective-permute-start | bytes 302600 | tf_op jit(solution)/shard_map/ppermute | solution.py:81
  33.8 84.9 %collective-permute-start.1 = (bf16[394,128]{1,0:T(8,128)(2,1)S(1)}, bf16[394,128]{1,0:T(8,128)(2,1)S(1)}, u32[]{:S(2)}, u32[]{:S(2)}) collective-permute-start(bf16[394,128]{1,0:T(8,128)(2,1)S(1)} %get-tuple-element.140), channel_id=1, source_target_pairs={{0,16},{8,24},{16,0},{24,8},{1,17},{9,25},{17,1},{25,9},{2,18},{10... | collective-permute-start | bytes 302600 | tf_op jit(solution)/shard_map/ppermute | solution.py:81
  97.3 10.8 %collective-permute-start.10 = (bf16[4,256,128]{2,1,0:T(8,128)(2,1)S(1)}, bf16[4,256,128]{2,1,0:T(8,128)(2,1)S(1)}, u32[]{:S(2)}, u32[]{:S(2)}) collective-permute-start(bf16[4,256,128]{2,1,0:T(8,128)(2,1)S(1)} %pad_maximum_fusion.7), channel_id=1, source_target_pairs={{0,16},{8,24},{16,0},{24,8},{1,17},{9,25},{17,1},{25,9},{2,18},{10... | collective-permute-start | bytes 786440 | tf_op jit(solution)/shard_map/ppermute | solution.py:86
  99.0 13.0 %collective-permute-start.11 = (bf16[4,256,128]{2,1,0:T(8,128)(2,1)S(1)}, bf16[4,256,128]{2,1,0:T(8,128)(2,1)S(1)}, u32[]{:S(2)}, u32[]{:S(2)}) collective-permute-start(bf16[4,256,128]{2,1,0:T(8,128)(2,1)S(1)} %pad_maximum_fusion.7), channel_id=1, source_target_pairs={{0,8},{8,0},{16,24},{24,16},{1,9},{9,1},{17,25},{25,17},{2,10},{10... | collective-permute-start | bytes 786440 | tf_op jit(solution)/shard_map/ppermute | solution.py:86
  100.5 16.6 %collective-permute-start.9 = (bf16[4,256,128]{2,1,0:T(8,128)(2,1)S(1)}, bf16[4,256,128]{2,1,0:T(8,128)(2,1)S(1)}, u32[]{:S(2)}, u32[]{:S(2)}) collective-permute-start(bf16[4,256,128]{2,1,0:T(8,128)(2,1)S(1)} %pad_maximum_fusion.7), channel_id=1, source_target_pairs={{0,24},{8,16},{16,8},{24,0},{1,25},{9,17},{17,9},{25,1},{2,26},{10... | collective-permute-start | bytes 786440 | tf_op jit(solution)/shard_map/ppermute | solution.py:86
  108.1 10.6 %collective-permute-start.2 = (bf16[394,128]{1,0:T(8,128)(2,1)S(1)}, bf16[394,128]{1,0:T(8,128)(2,1)S(1)}, u32[]{:S(2)}, u32[]{:S(2)}) collective-permute-start(bf16[394,128]{1,0:T(8,128)(2,1)S(1)} %get-tuple-element.139), channel_id=1, source_target_pairs={{0,8},{8,0},{16,24},{24,16},{1,9},{9,1},{17,25},{25,17},{2,10},{10... | collective-permute-start | bytes 302600 | tf_op jit(solution)/shard_map/ppermute | solution.py:81
  112.0 86.2 %collective-permute-start.19 = (bf16[32,128]{1,0:T(8,128)(2,1)}, bf16[32,128]{1,0:T(8,128)(2,1)}, u32[]{:S(2)}, u32[]{:S(2)}) collective-permute-start(bf16[32,128]{1,0:T(8,128)(2,1)} %bitcast.51), channel_id=1, source_target_pairs={{0,24},{8,16},{16,8},{24,0},{1,25},{9,17},{17,9},{25,1},{2,26},{10... | collective-permute-start | bytes 24584 | tf_op jit(solution)/shard_map/ppermute | solution.py:86
  117.4 2.7 collective-permute-start.12
  117.5 80.7 %collective-permute-start.20 = (bf16[32,128]{1,0:T(8,128)(2,1)}, bf16[32,128]{1,0:T(8,128)(2,1)}, u32[]{:S(2)}, u32[]{:S(2)}) collective-permute-start(bf16[32,128]{1,0:T(8,128)(2,1)} %bitcast.51), channel_id=1, source_target_pairs={{0,16},{8,24},{16,0},{24,8},{1,17},{9,25},{17,1},{25,9},{2,18},{10... | collective-permute-start | bytes 24584 | tf_op jit(solution)/shard_map/ppermute | solution.py:86
  144.4 20.8 %collective-permute-start.16 = (bf16[394,128]{1,0:T(8,128)(2,1)S(1)}, bf16[394,128]{1,0:T(8,128)(2,1)S(1)}, u32[]{:S(2)}, u32[]{:S(2)}) collective-permute-start(bf16[394,128]{1,0:T(8,128)(2,1)S(1)} %bitcast.468), channel_id=1, source_target_pairs={{0,24},{8,16},{16,8},{24,0},{1,25},{9,17},{17,9},{25,1},{2,26},{10... | collective-permute-start | bytes 302600 | tf_op jit(solution)/shard_map/ppermute | solution.py:81
  146.5 19.9 %collective-permute-start.17 = (bf16[394,128]{1,0:T(8,128)(2,1)S(1)}, bf16[394,128]{1,0:T(8,128)(2,1)S(1)}, u32[]{:S(2)}, u32[]{:S(2)}) collective-permute-start(bf16[394,128]{1,0:T(8,128)(2,1)S(1)} %bitcast.467), channel_id=1, source_target_pairs={{0,16},{8,24},{16,0},{24,8},{1,17},{9,25},{17,1},{25,9},{2,18},{10... | collective-permute-start | bytes 302600 | tf_op jit(solution)/shard_map/ppermute | solution.py:81
  147.3 19.2 %collective-permute-start.18 = (bf16[394,128]{1,0:T(8,128)(2,1)S(1)}, bf16[394,128]{1,0:T(8,128)(2,1)S(1)}, u32[]{:S(2)}, u32[]{:S(2)}) collective-permute-start(bf16[394,128]{1,0:T(8,128)(2,1)S(1)} %bitcast.469), channel_id=1, source_target_pairs={{0,8},{8,0},{16,24},{24,16},{1,9},{9,1},{17,25},{25,17},{2,10},{10... | collective-permute-start | bytes 302600 | tf_op jit(solution)/shard_map/ppermute | solution.py:81
  165.2 33.1 %collective-permute-start.21 = (bf16[32,128]{1,0:T(8,128)(2,1)}, bf16[32,128]{1,0:T(8,128)(2,1)S(1)}, u32[]{:S(2)}, u32[]{:S(2)}) collective-permute-start(bf16[32,128]{1,0:T(8,128)(2,1)} %bitcast.51), channel_id=1, source_target_pairs={{0,8},{8,0},{16,24},{24,16},{1,9},{9,1},{17,25},{25,17},{2,10},{10... | collective-permute-start | bytes 24584 | tf_op jit(solution)/shard_map/ppermute | solution.py:86
  178.9 34.8 %all-to-all-start.1 = ((bf16[32,120,128]{2,1,0:T(8,128)(2,1)}), bf16[32,120,128]{2,1,0:T(8,128)(2,1)}, u32[]{:S(2)}, u32[]{:S(2)}) async-start(bf16[32,120,128]{2,1,0:T(8,128)(2,1)} %bitcast.45), calls=%async_computation.1 | async-start | bytes 1966080 | tf_op jit(solution)/shard_map/all_to_all | solution.py:30
  197.4 75.0 %copy-start.73 = (f32[32]{0:T(128)}, f32[32]{0:T(128)S(1)}, u32[]{:S(2)}) copy-start(f32[32]{0:T(128)S(1)} %compare_convert_fusion) | copy-start | bytes 388
  215.7 32.3 %all-to-all-start.2 = ((bf16[32,120,128]{2,1,0:T(8,128)(2,1)}), bf16[32,120,128]{2,1,0:T(8,128)(2,1)S(1)}, u32[]{:S(2)}, u32[]{:S(2)}) async-start(bf16[32,120,128]{2,1,0:T(8,128)(2,1)} %bitcast.460), calls=%async_computation.2 | async-start | bytes 1966080 | tf_op jit(solution)/shard_map/all_to_all | solution.py:30
  244.2 28.2 %copy-start.32 = (f32[960,32]{0,1:T(8,128)}, f32[960,32]{0,1:T(8,128)S(1)}, u32[]{:S(2)}) copy-start(f32[960,32]{0,1:T(8,128)S(1)} %get-tuple-element.181) | copy-start | bytes 368644
  257.8 30.0 %all-to-all-start.3 = ((bf16[32,120,128]{2,1,0:T(8,128)(2,1)}), bf16[32,120,128]{2,1,0:T(8,128)(2,1)}, u32[]{:S(2)}, u32[]{:S(2)}) async-start(bf16[32,120,128]{2,1,0:T(8,128)(2,1)} %bitcast.63), calls=%async_computation.3 | async-start | bytes 1966080 | tf_op jit(solution)/shard_map/all_to_all | solution.py:30
  287.8 37.8 %all-to-all-start.4 = ((bf16[32,120,128]{2,1,0:T(8,128)(2,1)}), bf16[32,120,128]{2,1,0:T(8,128)(2,1)}, u32[]{:S(2)}, u32[]{:S(2)}) async-start(bf16[32,120,128]{2,1,0:T(8,128)(2,1)} %bitcast.75), calls=%async_computation.4 | async-start | bytes 1966080 | tf_op jit(solution)/shard_map/all_to_all | solution.py:30
  291.2 13.3 %collective-permute-start.22 = (bf16[394,128]{1,0:T(8,128)(2,1)S(1)}, bf16[394,128]{1,0:T(8,128)(2,1)S(1)}, u32[]{:S(2)}, u32[]{:S(2)}) collective-permute-start(bf16[394,128]{1,0:T(8,128)(2,1)S(1)} %get-tuple-element.135), channel_id=1, source_target_pairs={{0,24},{8,16},{16,8},{24,0},{1,25},{9,17},{17,9},{25,1},{2,26},{10... | collective-permute-start | bytes 302600 | tf_op jit(solution)/shard_map/ppermute | solution.py:81
  293.8 11.7 %collective-permute-start.23 = (bf16[394,128]{1,0:T(8,128)(2,1)S(1)}, bf16[394,128]{1,0:T(8,128)(2,1)S(1)}, u32[]{:S(2)}, u32[]{:S(2)}) collective-permute-start(bf16[394,128]{1,0:T(8,128)(2,1)S(1)} %get-tuple-element.134), channel_id=1, source_target_pairs={{0,16},{8,24},{16,0},{24,8},{1,17},{9,25},{17,1},{25,9},{2,18},{10... | collective-permute-start | bytes 302600 | tf_op jit(solution)/shard_map/ppermute | solution.py:81
  294.3 11.5 %collective-permute-start.24 = (bf16[394,128]{1,0:T(8,128)(2,1)S(1)}, bf16[394,128]{1,0:T(8,128)(2,1)S(1)}, u32[]{:S(2)}, u32[]{:S(2)}) collective-permute-start(bf16[394,128]{1,0:T(8,128)(2,1)S(1)} %get-tuple-element.133), channel_id=1, source_target_pairs={{0,8},{8,0},{16,24},{24,16},{1,9},{9,1},{17,25},{25,17},{2,10},{10... | collective-permute-start | bytes 302600 | tf_op jit(solution)/shard_map/ppermute | solution.py:81
  336.4 14.4 %collective-permute-start.25 = (bf16[394,128]{1,0:T(8,128)(2,1)}, bf16[394,128]{1,0:T(8,128)(2,1)}, u32[]{:S(2)}, u32[]{:S(2)}) collective-permute-start(bf16[394,128]{1,0:T(8,128)(2,1)} %get-tuple-element.138), channel_id=1, source_target_pairs={{0,24},{8,16},{16,8},{24,0},{1,25},{9,17},{17,9},{25,1},{2,26},{10... | collective-permute-start | bytes 302600 | tf_op jit(solution)/shard_map/ppermute | solution.py:81
  337.3 13.5 %collective-permute-start.26 = (bf16[394,128]{1,0:T(8,128)(2,1)}, bf16[394,128]{1,0:T(8,128)(2,1)}, u32[]{:S(2)}, u32[]{:S(2)}) collective-permute-start(bf16[394,128]{1,0:T(8,128)(2,1)} %get-tuple-element.137), channel_id=1, source_target_pairs={{0,16},{8,24},{16,0},{24,8},{1,17},{9,25},{17,1},{25,9},{2,18},{10... | collective-permute-start | bytes 302600 | tf_op jit(solution)/shard_map/ppermute | solution.py:81
  338.9 11.9 %collective-permute-start.27 = (bf16[394,128]{1,0:T(8,128)(2,1)}, bf16[394,128]{1,0:T(8,128)(2,1)}, u32[]{:S(2)}, u32[]{:S(2)}) collective-permute-start(bf16[394,128]{1,0:T(8,128)(2,1)} %get-tuple-element.136), channel_id=1, source_target_pairs={{0,8},{8,0},{16,24},{24,16},{1,9},{9,1},{17,25},{25,17},{2,10},{10... | collective-permute-start | bytes 302600 | tf_op jit(solution)/shard_map/ppermute | solution.py:81
  343.9 108.8 %all-to-all-start.5 = ((bf16[32,128,512]{2,1,0:T(8,128)(2,1)}), bf16[32,128,512]{2,1,0:T(8,128)(2,1)}, u32[]{:S(2)}, u32[]{:S(2)}) async-start(bf16[32,128,512]{2,1,0:T(8,128)(2,1)} %pad_maximum_fusion.1), calls=%async_computation.5 | async-start | bytes 8388608 | tf_op jit(solution)/shard_map/all_to_all | solution.py:30
  374.3 12.6 %collective-permute-start.31 = (bf16[4,292,512]{2,0,1:T(4,128)(2,1)}, bf16[4,292,512]{2,0,1:T(4,128)(2,1)}, u32[]{:S(2)}, u32[]{:S(2)}) collective-permute-start(bf16[4,292,512]{2,0,1:T(4,128)(2,1)} %bitcast.410), channel_id=1, source_target_pairs={{0,1},{1,0},{2,3},{3,2},{4,5},{5,4},{6,7},{7,6},{8,9},{9,8},{10,11... | collective-permute-start | bytes 3588104 | tf_op jit(solution)/shard_map/ppermute | solution.py:130
  376.9 21.2 %collective-permute-start.13 = (bf16[394,128]{1,0:T(8,128)(2,1)}, bf16[394,128]{1,0:T(8,128)(2,1)}, u32[]{:S(2)}, u32[]{:S(2)}) collective-permute-start(bf16[394,128]{1,0:T(8,128)(2,1)} %bitcast.419), channel_id=1, source_target_pairs={{0,24},{8,16},{16,8},{24,0},{1,25},{9,17},{17,9},{25,1},{2,26},{10... | collective-permute-start | bytes 302600 | tf_op jit(solution)/shard_map/ppermute | solution.py:81
  380.2 18.3 %collective-permute-start.14 = (bf16[394,128]{1,0:T(8,128)(2,1)}, bf16[394,128]{1,0:T(8,128)(2,1)}, u32[]{:S(2)}, u32[]{:S(2)}) collective-permute-start(bf16[394,128]{1,0:T(8,128)(2,1)} %bitcast.418), channel_id=1, source_target_pairs={{0,16},{8,24},{16,0},{24,8},{1,17},{9,25},{17,1},{25,9},{2,18},{10... | collective-permute-start | bytes 302600 | tf_op jit(solution)/shard_map/ppermute | solution.py:81
  381.4 19.6 %collective-permute-start.15 = (bf16[394,128]{1,0:T(8,128)(2,1)}, bf16[394,128]{1,0:T(8,128)(2,1)}, u32[]{:S(2)}, u32[]{:S(2)}) collective-permute-start(bf16[394,128]{1,0:T(8,128)(2,1)} %bitcast.417), channel_id=1, source_target_pairs={{0,8},{8,0},{16,24},{24,16},{1,9},{9,1},{17,25},{25,17},{2,10},{10... | collective-permute-start | bytes 302600 | tf_op jit(solution)/shard_map/ppermute | solution.py:81
  384.2 17.4 %collective-permute-start.28 = (bf16[394,128]{1,0:T(8,128)(2,1)S(1)}, bf16[394,128]{1,0:T(8,128)(2,1)S(1)}, u32[]{:S(2)}, u32[]{:S(2)}) collective-permute-start(bf16[394,128]{1,0:T(8,128)(2,1)S(1)} %bitcast.466), channel_id=1, source_target_pairs={{0,24},{8,16},{16,8},{24,0},{1,25},{9,17},{17,9},{25,1},{2,26},{10... | collective-permute-start | bytes 302600 | tf_op jit(solution)/shard_map/ppermute | solution.py:81
  386.9 20.7 %collective-permute-start.29 = (bf16[394,128]{1,0:T(8,128)(2,1)S(1)}, bf16[394,128]{1,0:T(8,128)(2,1)}, u32[]{:S(2)}, u32[]{:S(2)}) collective-permute-start(bf16[394,128]{1,0:T(8,128)(2,1)S(1)} %bitcast.465), channel_id=1, source_target_pairs={{0,16},{8,24},{16,0},{24,8},{1,17},{9,25},{17,1},{25,9},{2,18},{10... | collective-permute-start | bytes 302600 | tf_op jit(solution)/shard_map/ppermute | solution.py:81
  398.1 9.6 %collective-permute-start.30 = (bf16[394,128]{1,0:T(8,128)(2,1)S(1)}, bf16[394,128]{1,0:T(8,128)(2,1)S(1)}, u32[]{:S(2)}, u32[]{:S(2)}) collective-permute-start(bf16[394,128]{1,0:T(8,128)(2,1)S(1)} %bitcast.464), channel_id=1, source_target_pairs={{0,8},{8,0},{16,24},{24,16},{1,9},{9,1},{17,25},{25,17},{2,10},{10... | collective-permute-start | bytes 302600 | tf_op jit(solution)/shard_map/ppermute | solution.py:81
  398.4 18.6 %collective-permute-start.32 = (bf16[4,292,128]{2,1,0:T(8,128)(2,1)}, bf16[4,292,128]{2,1,0:T(8,128)(2,1)}, u32[]{:S(2)}, u32[]{:S(2)}) collective-permute-start(bf16[4,292,128]{2,1,0:T(8,128)(2,1)} %bitcast.413), channel_id=1, source_target_pairs={{0,24},{8,16},{16,8},{24,0},{1,25},{9,17},{17,9},{25,1},{2,26},{10... | collective-permute-start | bytes 897032 | tf_op jit(solution)/shard_map/ppermute | solution.py:81
  401.0 18.7 %collective-permute-start.33 = (bf16[4,292,128]{2,1,0:T(8,128)(2,1)}, bf16[4,292,128]{2,1,0:T(8,128)(2,1)}, u32[]{:S(2)}, u32[]{:S(2)}) collective-permute-start(bf16[4,292,128]{2,1,0:T(8,128)(2,1)} %bitcast.412), channel_id=1, source_target_pairs={{0,16},{8,24},{16,0},{24,8},{1,17},{9,25},{17,1},{25,9},{2,18},{10... | collective-permute-start | bytes 897032 | tf_op jit(solution)/shard_map/ppermute | solution.py:81
  401.6 20.4 %collective-permute-start.34 = (bf16[4,292,128]{2,1,0:T(8,128)(2,1)}, bf16[4,292,128]{2,1,0:T(8,128)(2,1)}, u32[]{:S(2)}, u32[]{:S(2)}) collective-permute-start(bf16[4,292,128]{2,1,0:T(8,128)(2,1)} %bitcast.411), channel_id=1, source_target_pairs={{0,8},{8,0},{16,24},{24,16},{1,9},{9,1},{17,25},{25,17},{2,10},{10... | collective-permute-start | bytes 897032 | tf_op jit(solution)/shard_map/ppermute | solution.py:81
  423.5 12.9 %collective-permute-start.35 = (bf16[292,128]{1,0:T(8,128)(2,1)S(1)}, bf16[292,128]{1,0:T(8,128)(2,1)S(1)}, u32[]{:S(2)}, u32[]{:S(2)}) collective-permute-start(bf16[292,128]{1,0:T(8,128)(2,1)S(1)} %get-tuple-element.154), channel_id=1, source_target_pairs={{0,2},{1,3},{2,0},{3,1},{4,6},{5,7},{6,4},{7,5},{8,10},{9,11},{10,... | collective-permute-start | bytes 224264 | tf_op jit(solution)/shard_map/ppermute | solution.py:111
  430.4 19.6 %collective-permute-start.36 = (bf16[292,128]{1,0:T(8,128)(2,1)S(1)}, bf16[292,128]{1,0:T(8,128)(2,1)S(1)}, u32[]{:S(2)}, u32[]{:S(2)}) collective-permute-start(bf16[292,128]{1,0:T(8,128)(2,1)S(1)} %get-tuple-element.156), channel_id=1, source_target_pairs={{0,4},{1,5},{2,6},{3,7},{4,0},{5,1},{6,2},{7,3},{8,12},{9,13},{10,... | collective-permute-start | bytes 224264 | tf_op jit(solution)/shard_map/ppermute | solution.py:111
  430.8 19.2 %collective-permute-start.37 = (bf16[292,128]{1,0:T(8,128)(2,1)S(1)}, bf16[292,128]{1,0:T(8,128)(2,1)S(1)}, u32[]{:S(2)}, u32[]{:S(2)}) collective-permute-start(bf16[292,128]{1,0:T(8,128)(2,1)S(1)} %get-tuple-element.155), channel_id=1, source_target_pairs={{0,6},{1,7},{2,4},{3,5},{4,2},{5,3},{6,0},{7,1},{8,14},{9,15},{10,... | collective-permute-start | bytes 224264 | tf_op jit(solution)/shard_map/ppermute | solution.py:111
  (74 other events, 471.9 us)
